TPU v7x, 32 devices: a whole 2x2x4 slice. The times are simulated.
32 devices in a mesh: src: 4 (over y, x), rcv: 8 (over z, core).
Axes of the slice: x: 2, y: 2, z: 4, core: 2. Of those that a mesh axis runs over, the one named last changes fastest.
Arguments:
- record: bfloat16 [1, 2, 6144, 6144], P(None, None, 'rcv', 'src'), may hold values from -6 to 6
- panel_offset: int32 [768], replicated, may hold values from 0 to 7
Outputs:
- primaries: bfloat16 [1, 2, 6144, 6144], P(None, None, 'rcv', 'src')
- multiples: bfloat16 [1, 2, 6144, 6144], P(None, None, 'rcv', 'src')
Inputs may be any that keep to these rules, and one draw needn't show every extreme that they name: Panel station j is 8 * j + panel_offset[j].
All inputs are finite; a program needn't handle non-finite values.
Results may differ from a plain program's by a relative error of at most 0.003.
The roundings to bfloat16 on the way count: a program that leaves them out, or rounds other values in their place, can miss the bound.
Values may be sent and summed in bfloat16 or wider, within the bound.
A program may use at most 128 MiB of HBM per device.

v0:
```python
import jax
import jax.numpy as jnp
from jax import lax
from jax.sharding import PartitionSpec as P

STRIDE = 8
REACH = 4
SWEEPS = 2


weight_eps = 1e-06


def extended(cells, sides, width, closed):
    for axis, dim in sides:
        count = lax.axis_size(axis)
        ends = count if closed else count - 1
        head = lax.slice_in_dim(cells, 0, width, axis=dim)
        tail = lax.slice_in_dim(cells, cells.shape[dim] - width, cells.shape[dim], axis=dim)
        cells = jnp.concatenate(
            [
                lax.ppermute(tail, axis, [(i, (i + 1) % count) for i in range(ends)]),
                cells,
                lax.ppermute(head, axis, [((i + 1) % count, i) for i in range(ends)]),
            ],
            axis=dim,
        )
    return cells


def reorder_keys(values, rcv_count, src_count):
    full_shape = values.shape
    grouped = values.reshape(
        full_shape[:-1] + (rcv_count, src_count, full_shape[-1] // (rcv_count * src_count))
    )
    return jnp.swapaxes(grouped, -3, -2).reshape(full_shape)


def average_pair(first_part, second_part):
    return ((first_part.astype(jnp.float32) + second_part.astype(jnp.float32)) * 0.5).astype(
        jnp.bfloat16
    )


def cross_dot(left_mat, right_mat):
    return lax.dot_general(
        left_mat, right_mat, (((2,), (2,)), ((0,), (0,))), preferred_element_type=jnp.float32
    )


def predict_block(right_side, left_side):
    right_real = right_side[:, 0]
    right_imag = right_side[:, 1]
    left_real = left_side[:, 0]
    left_imag = left_side[:, 1]
    pred_real = cross_dot(right_real, left_real) - cross_dot(right_imag, left_imag)
    pred_imag = cross_dot(right_real, left_imag) + cross_dot(right_imag, left_real)
    return jnp.stack([pred_real, pred_imag], axis=1)


def neighbour_sum(partial_terms, src_count, rcv_pos, rcv_count):
    freq_count, chan_count, rcv_cols, src_rows = partial_terms.shape
    run_len = rcv_cols // src_count
    runs_view = partial_terms.reshape(freq_count, chan_count, src_count, run_len, src_rows)
    padded = extended(runs_view.astype(jnp.bfloat16), (("rcv", 3),), REACH, True).astype(
        runs_view.dtype
    )
    lower_rim = padded[:, :, :, :REACH]
    middle = padded[:, :, :, REACH : REACH + run_len]
    upper_rim = padded[:, :, :, REACH + run_len :]
    zero_rim = jnp.zeros_like(lower_rim[:, :, :1])
    lower_rim = jnp.where(
        rcv_pos == 0, jnp.concatenate([zero_rim, lower_rim[:, :, :-1]], axis=2), lower_rim
    )
    upper_rim = jnp.where(
        rcv_pos == rcv_count - 1,
        jnp.concatenate([upper_rim[:, :, 1:], zero_rim], axis=2),
        upper_rim,
    )
    padded = jnp.concatenate([lower_rim, middle, upper_rim], axis=3)
    recv_total = padded[:, :, :, 0:run_len]
    for shift_pos in range(1, 2 * REACH + 1):
        recv_total = recv_total + padded[:, :, :, shift_pos : shift_pos + run_len]
    recv_total = recv_total.reshape(freq_count, chan_count, rcv_cols, src_rows)
    src_padded = extended(recv_total.astype(jnp.bfloat16), (("src", 3),), REACH, False).astype(
        recv_total.dtype
    )
    box_totals = src_padded[..., 0:src_rows]
    for shift_pos in range(1, 2 * REACH + 1):
        box_totals = box_totals + src_padded[..., shift_pos : shift_pos + src_rows]
    return box_totals


def run_sweeps(data_bf, pred_bf, summer):
    data_f32 = data_bf.astype(jnp.float32)
    pred_f32 = pred_bf.astype(jnp.float32)
    data_real = data_f32[:, 0]
    data_imag = data_f32[:, 1]
    pred_real = pred_f32[:, 0]
    pred_imag = pred_f32[:, 1]
    err_real = data_real
    err_imag = data_imag
    for sweep_step in range(SWEEPS):
        weight = 1.5 - jnp.tanh(err_real * err_real + err_imag * err_imag)
        partial_terms = jnp.stack(
            [
                weight * (pred_real * data_real + pred_imag * data_imag),
                weight * (pred_real * data_imag - pred_imag * data_real),
                weight * (pred_real * pred_real + pred_imag * pred_imag),
            ],
            axis=1,
        )
        box_totals = summer(partial_terms)
        denom = box_totals[:, 2] + weight_eps
        gain_real = box_totals[:, 0] / denom
        gain_imag = box_totals[:, 1] / denom
        err_real = data_real - (gain_real * pred_real - gain_imag * pred_imag)
        err_imag = data_imag - (gain_real * pred_imag + gain_imag * pred_real)
    return jnp.stack([err_real, err_imag], axis=1)


def shards(record, panel_offset):
    src_count = lax.axis_size("src")
    rcv_count = lax.axis_size("rcv")
    src_pos = lax.axis_index("src")
    rcv_pos = lax.axis_index("rcv")
    rcv_cols = record.shape[2]
    src_rows = record.shape[3]
    run_len = rcv_cols // src_count
    per_run = run_len // STRIDE
    panel_len = panel_offset.shape[0]
    run_ids = jnp.arange(src_count, dtype=jnp.int32)[:, None]
    within = jnp.arange(per_run, dtype=jnp.int32)[None, :]
    col_groups = (src_rows * run_ids + run_len * rcv_pos) // STRIDE + within
    col_index = (run_len * run_ids + STRIDE * within + jnp.take(panel_offset, col_groups)).reshape(
        -1
    )
    row_groups = jnp.arange(src_rows // STRIDE, dtype=jnp.int32)
    row_index = STRIDE * row_groups + jnp.take(
        panel_offset, src_rows // STRIDE * src_pos + row_groups
    )
    col_piece = jnp.swapaxes(jnp.take(record, col_index, axis=2), 2, 3)
    row_piece = jnp.take(record, row_index, axis=3)
    own_front = reorder_keys(
        lax.all_to_all(col_piece, "rcv", split_axis=2, concat_axis=3, tiled=True),
        rcv_count,
        src_count,
    )
    own_behind = lax.all_to_all(row_piece, "src", split_axis=2, concat_axis=3, tiled=True)
    owned_rows = average_pair(own_front, own_behind)
    right_side = lax.all_gather(owned_rows, "src", axis=2, tiled=True)
    prediction = predict_block(right_side, lax.all_gather(owned_rows, "rcv", axis=2, tiled=True))
    pred_round = lax.optimization_barrier(prediction.astype(jnp.bfloat16))
    multiples = (prediction * panel_len ** (-0.5)).astype(jnp.bfloat16)

    def runs_total(partial_terms):
        return neighbour_sum(partial_terms, src_count, rcv_pos, rcv_count)

    primaries = run_sweeps(record, pred_round, runs_total).astype(jnp.bfloat16)
    return (primaries, multiples)


def solution(mesh):
    in_specs = (P(None, None, "rcv", "src"), P())
    out_specs = (P(None, None, "rcv", "src"), P(None, None, "rcv", "src"))
    return jax.shard_map(shards, mesh=mesh, in_specs=in_specs, out_specs=out_specs, check_vma=False)
```

profile of v0, /device:TPU:0, one launch (start us, length us, event | category | flops | bytes accessed | tf_op | source)
XLA Modules:
  0.0 644.4 jit_solution(638596057733596686)
XLA Ops:
  9.1 12.4 %copy.100 = bf16[1,2,768,1536]{2,1,3,0:T(2,128)(2,1)} copy(bf16[1,2,768,1536]{3,2,1,0:T(8,128)(2,1)} %param.2) | data formatting | bytes 9437184 | tf_op args[0]
  34.3 9.4 %copy.119 = bf16[1,2,768,1536]{3,1,2,0:T(2,128)(2,1)} copy(bf16[1,2,768,1536]{3,2,1,0:T(8,128)(2,1)} %param.2) | data formatting | bytes 9437184 | tf_op args[0]
  58.5 19.1 %all-to-all-done = bf16[1,2,1536,96]{3,1,0,2:T(2,128)(2,1)S(1)} async-done(((bf16[1,2,1536,96]{3,1,0,2:T(2,128)(2,1)}), bf16[1,2,1536,96]{3,1,0,2:T(2,128)(2,1)S(1)}, u32[]{:S(2)}, u32[]{:S(2)}) %all-to-all-start) | async-done | bytes 589856 | tf_op jit(solution)/shard_map/all_to_all | solution.py:145
  86.8 7.4 %convert_element_type.211 = f32[1,2,768,1536]{3,2,1,0:T(8,128)} convert(bf16[1,2,768,1536]{3,2,1,0:T(8,128)(2,1)} %param.2) | non-fusion elementwise | flops 2359296 | bytes 14155776 | tf_op jit(solution)/shard_map/convert_element_type | solution.py:95
  94.2 28.9 %all-gather.3.cloned.1.call-done = bf16[1,2,768,768]{3,1,0,2:T(2,128)(2,1)} async-done(((bf16[1,2,192,768]{3,1,0,2:T(2,128)(2,1)}), bf16[1,2,768,768]{3,1,0,2:T(2,128)(2,1)}) %all-gather.3.cloned.1.call-update) | async-done | bytes 2359312 | tf_op jit(solution)/shard_map/all_gather | solution.py:151
  123.0 7.8 %fusion.42 = (bf16[1,1,768,768]{3,1,0,2:T(2,128)(2,1)S(1)}, bf16[1,1,768,768]{3,1,0,2:T(2,128)(2,1)}) fusion(bf16[1,2,768,768]{3,1,0,2:T(2,128)(2,1)} %all-gather.3.cloned.1.call-done), kind=kLoop, calls=%fused_computation.159 | loop fusion | bytes 4718592 | tf_op jit(solution)/shard_map/slice | solution.py:53
  130.8 46.1 %all-gather.5.cloned.1.call-done = bf16[1,2,1536,768]{3,1,0,2:T(2,128)(2,1)} async-done(((bf16[1,2,192,768]{3,1,0,2:T(2,128)(2,1)}), bf16[1,2,1536,768]{3,1,0,2:T(2,128)(2,1)}) %all-gather.5.cloned.1.call-update) | async-done | bytes 4718608 | tf_op jit(solution)/shard_map/all_gather | solution.py:152
  177.0 10.0 %fusion.41 = (bf16[1,1,1536,768]{3,1,0,2:T(2,128)(2,1)S(1)}, bf16[1,1,1536,768]{3,1,0,2:T(2,128)(2,1)S(1)}) fusion(bf16[1,2,1536,768]{3,1,0,2:T(2,128)(2,1)} %all-gather.5.cloned.1.call-done), kind=kLoop, calls=%fused_computation.158 | loop fusion | bytes 9437184 | tf_op jit(solution)/shard_map/slice | solution.py:54
  206.8 9.8 %multiply_convert_fusion.5 = (bf16[1,1,768,1536]{3,2,1,0:T(8,128)(2,1)}, f32[1,1,768,1536]{3,2,1,0:T(8,128)}, bf16[1,1,768,1536]{3,2,1,0:T(8,128)(2,1)}, bf16[1,1,768,1536]{3,2,1,0:T(8,128)(2,1)}, f32[1,1,768,1536]{3,2,1,0:T(8,128)}) fusion(f32[1,2,768,1536]{3,2,1,0:T(8,128)S(1)} %bitcast.86, f32[1,2,768,1536]{3,2,1,0:T(8,128)S(1)} %convert_element_type.223), kind=kLoop, calls=%fused_computation.93 | loop fusion | flops 22413312 | bytes 35389440 | tf_op jit(solution)/shard_map/convert.31
  225.4 7.6 %maximum_convert_fusion = f32[1,3,4,200,1536]{4,3,2,1,0:T(8,128)} fusion(bf16[1,3,4,4,1536]{4,3,2,1,0:T(4,128)(2,1)S(1)} %collective-permute-done.1, bf16[1,3,4,192,1536]{4,3,2,1,0:T(8,128)(2,1)S(1)} %maximum_bitcast_fusion, bf16[1,3,4,4,1536]{4,3,2,1,0:T(4,128)(2,1)S(1)} %collective-permute-done), kind=kLoop, calls=%fused_computation.73 | loop fusion | flops 22118400 | bytes 22118400 | tf_op jit(solution)/shard_map/convert_element_type | solution.py:65
  233.0 12.7 %slice.300 = f32[1,3,4,192,1536]{4,3,2,1,0:T(8,128)} slice(f32[1,3,4,200,1536]{4,3,2,1,0:T(8,128)} %maximum_convert_fusion), slice={[0:1], [0:3], [0:4], [4:196], [0:1536]} | slice | bytes 28311552 | tf_op jit(solution)/shard_map/slice | solution.py:69
  249.0 54.5 %fusion.18 = bf16[1,3,4,192,1536]{4,3,2,1,0:T(8,128)(2,1)S(1)} fusion(f32[1,3,4,4,1536]{4,3,2,1,0:T(4,128)S(1)} %get-tuple-element.18, f32[1,3,4,192,1536]{4,3,2,1,0:T(8,128)} %slice.300, f32[1,3,4,4,1536]{4,3,2,1,0:T(4,128)S(1)} %get-tuple-element.17), kind=kLoop, calls=%fused_computation.34 | loop fusion | flops 60162048 | bytes 21823488 | tf_op jit(solution)/shard_map/convert_element_type | solution.py:85
  314.9 14.1 %concatenate.151 = bf16[1,3,768,1544]{3,2,1,0:T(8,128)(2,1)} concatenate(bf16[1,3,768,4]{3,2,1,0:T(8,128)(2,1)S(1)} %copy.94, bf16[1,3,768,1536]{3,2,1,0:T(8,128)(2,1)} %bitcast.90, bf16[1,3,768,4]{3,2,1,0:T(8,128)(2,1)S(1)} %copy.95), dimensions={3} | concatenate | bytes 14229504 | tf_op jit(solution)/shard_map/concatenate | solution.py:20
  329.0 9.4 %convert_element_type.227 = f32[1,3,768,1544]{3,2,1,0:T(8,128)} convert(bf16[1,3,768,1544]{3,2,1,0:T(8,128)(2,1)} %concatenate.151) | non-fusion elementwise | flops 3557376 | bytes 21344256 | tf_op jit(solution)/shard_map/convert_element_type | solution.py:85
  338.4 67.0 %slice_add_fusion.8 = f32[1,3,768,1536]{3,2,1,0:T(8,128)} fusion(f32[1,3,768,1544]{3,2,1,0:T(8,128)} %convert_element_type.227), kind=kLoop, calls=%fused_computation.58 | loop fusion | flops 28311552 | bytes 141557760 | tf_op jit(solution)/shard_map/add | solution.py:90
  405.5 17.3 %multiply_convert_fusion.3 = (bf16[1,1,768,1536]{3,2,1,0:T(8,128)(2,1)}, f32[1,1,768,1536]{3,2,1,0:T(8,128)}) fusion(f32[1,1,768,1536]{3,2,1,0:T(8,128)} %get-tuple-element.12, f32[1,2,768,1536]{3,2,1,0:T(8,128)} %convert_element_type.211, f32[1,2,768,1536]{3,2,1,0:T(8,128)} %copy-done.2, f32[1,3,768,1536]{3,2,1,0:T(8,128)} %slice_add_fusion.8), kind=kLoop, calls=%fused_computation.89 | loop fusion | flops 20054016 | bytes 44826624 | tf_op jit(solution)/shard_map/convert.20
  435.1 7.6 %maximum_convert_fusion.1 = f32[1,3,4,200,1536]{4,3,2,1,0:T(8,128)} fusion(bf16[1,3,4,4,1536]{4,3,2,1,0:T(4,128)(2,1)S(1)} %collective-permute-done.5, bf16[1,3,4,192,1536]{4,3,2,1,0:T(8,128)(2,1)S(1)} %maximum_bitcast_fusion.1, bf16[1,3,4,4,1536]{4,3,2,1,0:T(4,128)(2,1)S(1)} %collective-permute-done.4), kind=kLoop, calls=%fused_computation.74 | loop fusion | flops 22118400 | bytes 22118400 | tf_op jit(solution)/shard_map/convert_element_type | solution.py:65
  442.6 12.7 %slice.327 = f32[1,3,4,192,1536]{4,3,2,1,0:T(8,128)} slice(f32[1,3,4,200,1536]{4,3,2,1,0:T(8,128)} %maximum_convert_fusion.1), slice={[0:1], [0:3], [0:4], [4:196], [0:1536]} | slice | bytes 28311552 | tf_op jit(solution)/shard_map/slice | solution.py:69
  458.6 54.1 %fusion.3 = bf16[1,3,4,192,1536]{4,3,2,1,0:T(8,128)(2,1)S(1)} fusion(f32[1,3,4,4,1536]{4,3,2,1,0:T(4,128)S(1)} %get-tuple-element.14, f32[1,3,4,192,1536]{4,3,2,1,0:T(8,128)} %slice.327, f32[1,3,4,4,1536]{4,3,2,1,0:T(4,128)S(1)} %get-tuple-element.13), kind=kLoop, calls=%fused_computation.19 | loop fusion | flops 60162048 | bytes 21823488 | tf_op jit(solution)/shard_map/convert_element_type | solution.py:85
  522.4 7.2 %multiply_convert_fusion = bf16[1,2,768,1536]{3,2,1,0:T(8,128)(2,1)} fusion(f32[1,1,768,1536]{3,2,1,0:T(8,128)} %add_bitcast_fusion, f32[1,1,768,1536]{3,2,1,0:T(8,128)} %copy-done.13), kind=kLoop, calls=%fused_computation.71 | loop fusion | flops 7077888 | bytes 14155776 | tf_op jit(solution)/shard_map/convert_element_type | solution.py:154
  530.3 14.1 %concatenate.158 = bf16[1,3,768,1544]{3,2,1,0:T(8,128)(2,1)} concatenate(bf16[1,3,768,4]{3,2,1,0:T(8,128)(2,1)S(1)} %copy.98, bf16[1,3,768,1536]{3,2,1,0:T(8,128)(2,1)} %bitcast.88, bf16[1,3,768,4]{3,2,1,0:T(8,128)(2,1)S(1)} %copy.99), dimensions={3} | concatenate | bytes 14229504 | tf_op jit(solution)/shard_map/concatenate | solution.py:20
  544.5 9.6 %convert_element_type.231 = f32[1,3,768,1544]{3,2,1,0:T(8,128)} convert(bf16[1,3,768,1544]{3,2,1,0:T(8,128)(2,1)} %concatenate.158) | non-fusion elementwise | flops 3557376 | bytes 21344256 | tf_op jit(solution)/shard_map/convert_element_type | solution.py:85
  554.0 68.1 %slice_add_fusion = f32[1,3,768,1536]{3,2,1,0:T(8,128)} fusion(f32[1,3,768,1544]{3,2,1,0:T(8,128)} %convert_element_type.231), kind=kLoop, calls=%fused_computation.46 | loop fusion | flops 28311552 | bytes 141557760 | tf_op jit(solution)/shard_map/add | solution.py:90
  622.1 12.4 %subtract_convert_fusion.1 = (bf16[1,1,768,1536]{3,2,1,0:T(8,128)(2,1)S(1)}, bf16[1,1,768,1536]{3,2,1,0:T(8,128)(2,1)S(1)}) fusion(f32[1,2,768,1536]{3,2,1,0:T(8,128)} %convert_element_type.211, f32[1,2,768,1536]{3,2,1,0:T(8,128)} %copy-done.2, f32[1,3,768,1536]{3,2,1,0:T(8,128)} %slice_add_fusion), kind=kLoop, calls=%fused_computation.86 | loop fusion | flops 15335424 | bytes 37748736 | tf_op jit(solution)/shard_map/convert.7
  (134 shorter events, 109.9 us)
Async XLA Ops:
  28.5 23.2 %all-to-all-start.1 = ((bf16[1,2,768,192]{3,1,0,2:T(2,128)(2,1)}), bf16[1,2,768,192]{3,1,0,2:T(2,128)(2,1)S(1)}, u32[]{:S(2)}, u32[]{:S(2)}) async-start(bf16[1,2,768,192]{3,1,0,2:T(2,128)(2,1)} %copy.83), calls=%async_computation.1 | async-start | bytes 1572864 | tf_op jit(solution)/shard_map/all_to_all | solution.py:149
  51.7 25.9 %all-to-all-start = ((bf16[1,2,1536,96]{3,1,0,2:T(2,128)(2,1)}), bf16[1,2,1536,96]{3,1,0,2:T(2,128)(2,1)S(1)}, u32[]{:S(2)}, u32[]{:S(2)}) async-start(bf16[1,2,1536,96]{3,1,0,2:T(2,128)(2,1)} %copy.78), calls=%async_computation | async-start | bytes 1572864 | tf_op jit(solution)/shard_map/all_to_all | solution.py:145
  56.6 66.4 %all-gather.3.cloned.1.call-start = ((), (), s32[]{:S(2)}) async-start(), calls=%async_computation.2 | async-start | bytes 2949120 | tf_op jit(solution)/shard_map/all_gather | solution.py:151
  86.0 91.0 %all-gather.5.cloned.1.call-start = ((), (), s32[]{:S(2)}) async-start(), calls=%async_computation.3 | async-start | bytes 5308416 | tf_op jit(solution)/shard_map/all_gather | solution.py:152
  177.0 10.1 %copy-start.14 = (bf16[1,1,768,768]{3,1,0,2:T(2,128)(2,1)S(1)}, bf16[1,1,768,768]{3,1,0,2:T(2,128)(2,1)}, u32[]{:S(2)}) copy-start(bf16[1,1,768,768]{3,1,0,2:T(2,128)(2,1)} %get-tuple-element.34) | copy-start | bytes 3538948
  193.2 4.2 copy-start.13
  197.4 9.3 %slice-start.3 = ((s8[9437184]{0:T(1024)(128)(4,1)}), s8[4194304]{0:T(1024)(128)(4,1)S(1)}, s32[]{:S(2)}) async-start(s8[9437184]{0:T(1024)(128)(4,1)} %bitcast.85), calls=%async_computation.7 | async-start | bytes 8388608
  197.4 9.3 %slice-start.4 = ((s8[9437184]{0:T(1024)(128)(4,1)}), s8[4194304]{0:T(1024)(128)(4,1)S(1)}, s32[]{:S(2)}) async-start(s8[9437184]{0:T(1024)(128)(4,1)} %bitcast.85), calls=%async_computation.8 | async-start | bytes 8388608
  206.8 9.8 %copy-start.2 = (f32[1,2,768,1536]{3,2,1,0:T(8,128)}, f32[1,2,768,1536]{3,2,1,0:T(8,128)S(1)}, u32[]{:S(2)}) copy-start(f32[1,2,768,1536]{3,2,1,0:T(8,128)S(1)} %convert_element_type.223) | copy-start | bytes 28311556
  216.5 5.0 copy-start.10
  216.6 5.0 copy-start.11
  216.6 5.0 copy-start.12
  218.0 7.4 %collective-permute-start = (bf16[1,3,4,4,1536]{4,3,2,1,0:T(4,128)(2,1)S(1)}, bf16[1,3,4,4,1536]{4,3,2,1,0:T(4,128)(2,1)S(1)}, u32[]{:S(2)}, u32[]{:S(2)}) collective-permute-start(bf16[1,3,4,4,1536]{4,3,2,1,0:T(4,128)(2,1)S(1)} %get-tuple-element.27), channel_id=1, source_target_pairs={{0,1},{1,2},{2,3},{3,4},{4,5},{5,6},{6,7},{7,0},{8,9},{9,10},{10,1... | collective-permute-start | bytes 442376 | tf_op jit(solution)/shard_map/ppermute | solution.py:22
  218.3 7.1 %collective-permute-start.1 = (bf16[1,3,4,4,1536]{4,3,2,1,0:T(4,128)(2,1)S(1)}, bf16[1,3,4,4,1536]{4,3,2,1,0:T(4,128)(2,1)S(1)}, u32[]{:S(2)}, u32[]{:S(2)}) collective-permute-start(bf16[1,3,4,4,1536]{4,3,2,1,0:T(4,128)(2,1)S(1)} %get-tuple-element.28), channel_id=1, source_target_pairs={{1,0},{2,1},{3,2},{4,3},{5,4},{6,5},{7,6},{0,7},{9,8},{10,9},{11,1... | collective-permute-start | bytes 442376 | tf_op jit(solution)/shard_map/ppermute | solution.py:24
  306.9 6.3 collective-permute-start.3
  308.5 6.0 collective-permute-start.2
  405.4 17.3 %slice-start = ((s8[9437184]{0:T(1024)(128)(4,1)}), s8[4194304]{0:T(1024)(128)(4,1)S(1)}, s32[]{:S(2)}) async-start(s8[9437184]{0:T(1024)(128)(4,1)} %bitcast.83), calls=%async_computation.4 | async-start | bytes 8388608
  405.5 17.3 %slice-start.1 = ((s8[9437184]{0:T(1024)(128)(4,1)}), s8[4194304]{0:T(1024)(128)(4,1)S(1)}, s32[]{:S(2)}) async-start(s8[9437184]{0:T(1024)(128)(4,1)} %bitcast.83), calls=%async_computation.5 | async-start | bytes 8388608
  405.5 17.3 %slice-start.2 = ((s8[9437184]{0:T(1024)(128)(4,1)}), s8[1048576]{0:T(1024)(128)(4,1)S(1)}, s32[]{:S(2)}) async-start(s8[9437184]{0:T(1024)(128)(4,1)} %bitcast.83), calls=%async_computation.6 | async-start | bytes 2097152
  422.8 4.6 copy-start.9
  427.5 6.7 %collective-permute-start.4 = (bf16[1,3,4,4,1536]{4,3,2,1,0:T(4,128)(2,1)S(1)}, bf16[1,3,4,4,1536]{4,3,2,1,0:T(4,128)(2,1)S(1)}, u32[]{:S(2)}, u32[]{:S(2)}) collective-permute-start(bf16[1,3,4,4,1536]{4,3,2,1,0:T(4,128)(2,1)S(1)} %get-tuple-element.23), channel_id=1, source_target_pairs={{0,1},{1,2},{2,3},{3,4},{4,5},{5,6},{6,7},{7,0},{8,9},{9,10},{10,1... | collective-permute-start | bytes 442376 | tf_op jit(solution)/shard_map/ppermute | solution.py:22
  427.6 6.7 %collective-permute-start.5 = (bf16[1,3,4,4,1536]{4,3,2,1,0:T(4,128)(2,1)S(1)}, bf16[1,3,4,4,1536]{4,3,2,1,0:T(4,128)(2,1)S(1)}, u32[]{:S(2)}, u32[]{:S(2)}) collective-permute-start(bf16[1,3,4,4,1536]{4,3,2,1,0:T(4,128)(2,1)S(1)} %get-tuple-element.24), channel_id=1, source_target_pairs={{1,0},{2,1},{3,2},{4,3},{5,4},{6,5},{7,6},{0,7},{9,8},{10,9},{11,1... | collective-permute-start | bytes 442376 | tf_op jit(solution)/shard_map/ppermute | solution.py:24
  516.4 13.6 %collective-permute-start.6 = (bf16[1,3,768,4]{2,3,1,0:T(4,128)(2,1)S(1)}, bf16[1,3,768,4]{2,3,1,0:T(4,128)(2,1)S(1)}, u32[]{:S(2)}, u32[]{:S(2)}) collective-permute-start(bf16[1,3,768,4]{2,3,1,0:T(4,128)(2,1)S(1)} %copy.96), channel_id=1, source_target_pairs={{0,8},{8,16},{16,24},{1,9},{9,17},{17,25},{2,10},{10,18},{18,26},{... | collective-permute-start | bytes 55304 | tf_op jit(solution)/shard_map/ppermute | solution.py:22
  520.9 8.8 %collective-permute-start.7 = (bf16[1,3,768,4]{2,3,1,0:T(4,128)(2,1)S(1)}, bf16[1,3,768,4]{2,3,1,0:T(4,128)(2,1)S(1)}, u32[]{:S(2)}, u32[]{:S(2)}) collective-permute-start(bf16[1,3,768,4]{2,3,1,0:T(4,128)(2,1)S(1)} %copy.97), channel_id=1, source_target_pairs={{8,0},{16,8},{24,16},{9,1},{17,9},{25,17},{10,2},{18,10},{26,18},{... | collective-permute-start | bytes 55304 | tf_op jit(solution)/shard_map/ppermute | solution.py:24
  (9 other events, 24.8 us)
Sparse Core Ops, SparseCore 0:
  86.1 36.8 all-gather.2
  125.2 51.6 all-gather.4
where the time goes:
time: 656 us; the launch traced here: 644 us
  other arithmetic  355 us (54%)
  local copies, waits for them, and re-layouts  133 us (20%)
  waiting for transfers between devices  101 us (15%)
  starting transfers between devices  29.7 us (5%)
  between operations  15 us (2%)
  matrix products  10.3 us (2%)
    add x2, other arithmetic, neighbour_sum(): box_totals = box_totals + src_padded[..., shift_pos:shift_pos + src_rows]  135 us
    convert_element_type x2, other arithmetic, neighbour_sum(): recv_total.astype(jnp.bfloat16)  109 us
    all_gather x1, waiting for transfers between devices, shards(): lax.all_gather(owned_rows, 'rcv', axis=2, tiled=True)  46.1 us
    another operation x4, other arithmetic  44.1 us
    unnamed x44, local copies, waits for them, and re-layouts  34.9 us
    all_gather x1, waiting for transfers between devices, shards(): right_side = lax.all_gather(owned_rows, 'src', axis=2, tiled=True)  28.9 us
    concatenate x2, local copies, waits for them, and re-layouts, extended(): jnp.concatenate([lax.ppermute(tail, axis, [(i, (i + 1) % count) for i in...  28.3 us
    slice x2, local copies, waits for them, and re-layouts, neighbour_sum(): middle = padded[:, :, :, REACH:REACH + run_len]  25.5 us
  transfers between devices with their start and end apart: 12, of which 6 were waited for; matrix products, arithmetic and copies ran while one was open for 7% of the time, Pallas kernels for 0%

commit v1 on v0

--- a/solution.py
+++ b/solution.py
@@ -1,6 +1,10 @@
+import functools
+
 import jax
 import jax.numpy as jnp
 from jax import lax
+from jax.experimental import pallas as pl
+from jax.experimental.pallas import tpu as pltpu
 from jax.sharding import PartitionSpec as P
 
 STRIDE = 8
@@ -119,7 +123,7 @@
     return jnp.stack([err_real, err_imag], axis=1)
 
 
-def shards(record, panel_offset):
+def plain_shards(record, panel_offset):
     src_count = lax.axis_size("src")
     rcv_count = lax.axis_size("rcv")
     src_pos = lax.axis_index("src")
@@ -159,6 +163,306 @@
     primaries = run_sweeps(record, pred_round, runs_total).astype(jnp.bfloat16)
     return (primaries, multiples)
 
+HALO = 2 * REACH
+
+
+def wide_spans(width):
+    spans = [(start, 256) for start in range(0, width - 255, 256)]
+    done = 256 * (width // 256)
+    return spans + ([(done, width - done)] if done < width else [])
+
+
+def band(shape, shift, period):
+    rows = lax.broadcasted_iota(jnp.int32, shape, 0)
+    cols = lax.broadcasted_iota(jnp.int32, shape, 1) + shift
+    gap = jnp.abs(rows - cols)
+    if period:
+        gap = jnp.minimum(gap, period - gap)
+    return jnp.where(gap <= REACH, 1.0, 0.0).astype(jnp.bfloat16)
+
+
+def sweep_kernel(
+    scale, record_ref, rim_ref, side_ref, right_ref, left_ref, prim_ref, mult_ref,
+    left_all, right_all, data, pred32, predb, terms, partial, totals, row_band, lane_band
+):
+    runs_len = record_ref.shape[2]
+    src_rows = record_ref.shape[3]
+    owners = left_ref.shape[0]
+    rows = runs_len + 2 * HALO
+    width = src_rows + 128
+    panel = left_ref.shape[3]
+    f32, bf = jnp.float32, jnp.bfloat16
+
+    @pl.when(pl.program_id(0) == 0)
+    def _():
+        row_band[...] = band((rows, rows), 0, rows)
+        lane_band[...] = band((512, 256), 128, 0)
+        left_all[src_rows:, :] = jnp.zeros((128, 2 * panel), bf)
+        for chan in range(2):
+            lanes = slice(chan * panel, (chan + 1) * panel)
+            for owner in range(owners):
+                left_all[owner * runs_len : (owner + 1) * runs_len, lanes] = left_ref[
+                    owner, chan, :runs_len
+                ]
+            after = left_ref[owners - 1, chan, runs_len:]
+            before = left_ref[0, chan, runs_len:]
+            spot = lax.broadcasted_iota(jnp.int32, after.shape, 0)
+            zero = jnp.zeros_like(after)
+            left_all[src_rows : src_rows + 2 * HALO, lanes] = jnp.where(spot < HALO, after, zero)
+            left_all[width - 2 * HALO : width, lanes] = jnp.where(spot >= HALO, before, zero)
+
+    for chan in range(2):
+        data[chan, :runs_len, :src_rows] = record_ref[0, chan]
+        data[chan, runs_len:, :src_rows] = rim_ref[chan, 0]
+        data[chan, :, src_rows:] = side_ref[chan, 0]
+    right_real = right_ref[0, 0]
+    right_imag = right_ref[0, 1]
+    right_all[:rows, :panel] = right_real
+    right_all[:rows, panel:] = -right_imag
+    right_all[rows:, :panel] = right_imag
+    right_all[rows:, panel:] = right_real
+    for start, size in wide_spans(width):
+        pred32[:, start : start + size] = lax.dot_general(
+            right_all[...],
+            left_all[start : start + size, :],
+            (((1,), (1,)), ((), ())),
+            preferred_element_type=f32,
+        )
+
+    def put_terms(at, lanes, err, here, guess):
+        weight = 1.5 - jnp.tanh(err[0] * err[0] + err[1] * err[1])
+        parts = (
+            guess[0] * here[0] + guess[1] * here[1],
+            guess[0] * here[1] - guess[1] * here[0],
+            guess[0] * guess[0] + guess[1] * guess[1],
+        )
+        for index, part in enumerate(parts):
+            terms[index, at, lanes] = (weight * part).astype(bf)
+
+    def new_err(at, lanes):
+        here = [data[chan, at, lanes].astype(f32) for chan in range(2)]
+        guess = [predb[chan, at, lanes].astype(f32) for chan in range(2)]
+        inverse = 1.0 / (totals[2, at, lanes] + weight_eps)
+        gain_real = totals[0, at, lanes] * inverse
+        gain_imag = totals[1, at, lanes] * inverse
+        err = (
+            here[0] - (gain_real * guess[0] - gain_imag * guess[1]),
+            here[1] - (gain_real * guess[1] + gain_imag * guess[0]),
+        )
+        return err, here, guess
+
+    def box():
+        for index in range(3):
+            for start, size in wide_spans(width):
+                partial[index, :, 128 + start : 128 + start + size] = jnp.dot(
+                    row_band[...], terms[index, :, start : start + size], preferred_element_type=f32
+                ).astype(bf)
+            partial[index, :, :128] = partial[index, :, width : width + 128]
+            partial[index, :, width + 128 :] = partial[index, :, 128:256]
+        for index in range(3):
+            for start, size in wide_spans(width):
+                totals[index, :, start : start + size] = jnp.dot(
+                    partial[index, :, start : start + size + 256],
+                    lane_band[: size + 256, :size],
+                    preferred_element_type=f32,
+                )
+
+    @pl.loop(0, rows // 16)
+    def _(step):
+        at = pl.ds(pl.multiple_of(step * 16, 16), 16)
+        at_imag = pl.ds(pl.multiple_of(rows + step * 16, 16), 16)
+        for block in range(width // 128):
+            lanes = slice(block * 128, (block + 1) * 128)
+            here = [data[chan, at, lanes].astype(f32) for chan in range(2)]
+            guess = []
+            for chan, spot in enumerate((at, at_imag)):
+                rounded = pred32[spot, lanes].astype(bf)
+                predb[chan, at, lanes] = rounded
+                guess.append(rounded.astype(f32))
+            put_terms(at, lanes, here, here, guess)
+
+    @pl.loop(0, runs_len // 16)
+    def _(step):
+        at = pl.ds(pl.multiple_of(step * 16, 16), 16)
+        at_imag = pl.ds(pl.multiple_of(rows + step * 16, 16), 16)
+        for block in range(src_rows // 128):
+            lanes = slice(block * 128, (block + 1) * 128)
+            mult_ref[0, 0, at, lanes] = (pred32[at, lanes] * scale).astype(bf)
+            mult_ref[0, 1, at, lanes] = (pred32[at_imag, lanes] * scale).astype(bf)
+
+    for sweep_step in range(SWEEPS - 1):
+        box()
+
+        @pl.loop(0, rows // 16)
+        def _(step):
+            at = pl.ds(pl.multiple_of(step * 16, 16), 16)
+            for block in range(width // 128):
+                lanes = slice(block * 128, (block + 1) * 128)
+                put_terms(at, lanes, *new_err(at, lanes))
+
+    box()
+
+    @pl.loop(0, runs_len // 16)
+    def _(step):
+        at = pl.ds(pl.multiple_of(step * 16, 16), 16)
+        for block in range(src_rows // 128):
+            lanes = slice(block * 128, (block + 1) * 128)
+            err, _, _ = new_err(at, lanes)
+            prim_ref[0, 0, at, lanes] = err[0].astype(bf)
+            prim_ref[0, 1, at, lanes] = err[1].astype(bf)
+
+
+def sweep_call(record, rims, sides, right, left):
+    _, _, rcv_cols, src_rows = record.shape
+    runs = right.shape[0]
+    run_len = rcv_cols // runs
+    rows = run_len + 2 * HALO
+    width = src_rows + 128
+    panel = left.shape[3]
+    f32, bf = jnp.float32, jnp.bfloat16
+    out = jax.ShapeDtypeStruct(record.shape, bf)
+    tile = pl.BlockSpec((1, 2, run_len, src_rows), lambda r: (0, 0, r, 0))
+    return pl.pallas_call(
+        functools.partial(sweep_kernel, panel ** (-0.5)),
+        grid=(runs,),
+        out_shape=(out, out),
+        in_specs=[
+            tile,
+            pl.BlockSpec((2, 1, 2 * HALO, src_rows), lambda r: (0, r, 0, 0)),
+            pl.BlockSpec((2, 1, rows, 128), lambda r: (0, r, 0, 0)),
+            pl.BlockSpec((1, 2, rows, panel), lambda r: (r, 0, 0, 0)),
+            pl.BlockSpec(left.shape, lambda r: (0, 0, 0, 0), pipeline_mode=pl.Buffered(1)),
+        ],
+        out_specs=(tile, tile),
+        scratch_shapes=[
+            pltpu.VMEM((width, 2 * panel), bf),
+            pltpu.VMEM((2 * rows, 2 * panel), bf),
+            pltpu.VMEM((2, rows, width), bf),
+            pltpu.VMEM((2 * rows, width), f32),
+            pltpu.VMEM((2, rows, width), bf),
+            pltpu.VMEM((3, rows, width), bf),
+            pltpu.VMEM((3, rows, width + 256), bf),
+            pltpu.VMEM((3, rows, width), f32),
+            pltpu.VMEM((rows, rows), bf),
+            pltpu.VMEM((512, 256), bf),
+        ],
+        compiler_params=pltpu.CompilerParams(vmem_limit_bytes=56 * 1024 * 1024),
+        cost_estimate=pl.CostEstimate(
+            flops=20_000_000_000, bytes_accessed=4 * record.size * 2, transcendentals=2 * record.size
+        ),
+    )(record, rims, sides, right, left)
+
+
+def average_kernel(front_ref, behind_ref, own_ref):
+    srcs = behind_ref.shape[1]
+    rcvs = front_ref.shape[1]
+    panel = own_ref.shape[2]
+    each = panel // (srcs * rcvs)
+    f32, bf = jnp.float32, jnp.bfloat16
+
+    for chan in range(2):
+        total = jnp.zeros(own_ref.shape[1:], f32)
+        for rcv in range(rcvs):
+            shape = (srcs * each, panel)
+            index = lax.broadcasted_iota(jnp.int32, shape, 0)
+            column = lax.broadcasted_iota(jnp.int32, shape, 1)
+            aim = index // each * (rcvs * each) + rcv * each + index % each
+            pick = jnp.where(column == aim, 1.0, 0.0).astype(bf)
+            total = total + jnp.dot(front_ref[chan, rcv], pick, preferred_element_type=f32)
+        for src in range(srcs):
+            shape = (rcvs * each, panel)
+            index = lax.broadcasted_iota(jnp.int32, shape, 0)
+            column = lax.broadcasted_iota(jnp.int32, shape, 1)
+            pick = jnp.where(column == index + src * rcvs * each, 1.0, 0.0).astype(bf)
+            total = total + jnp.dot(behind_ref[chan, src], pick, preferred_element_type=f32)
+        own_ref[chan] = (total * 0.5).astype(bf)
+
+
+def average_call(front, behind, panel):
+    return pl.pallas_call(
+        average_kernel,
+        out_shape=jax.ShapeDtypeStruct((2, front.shape[2], panel), jnp.bfloat16),
+        in_specs=[pl.BlockSpec(memory_space=pltpu.VMEM)] * 2,
+        out_specs=pl.BlockSpec(memory_space=pltpu.VMEM),
+        compiler_params=pltpu.CompilerParams(vmem_limit_bytes=32 * 1024 * 1024),
+    )(front, behind)
+
+
+def panel_places(panel_offset, src_count, rcv_count, src_pos, rcv_pos, run_len, src_rows):
+    per_run = run_len // STRIDE
+    run_ids = jnp.arange(src_count, dtype=jnp.int32)[:, None]
+    within = jnp.arange(per_run, dtype=jnp.int32)[None, :]
+    by_block = panel_offset.reshape(src_count, rcv_count, per_run)
+    mine = lax.dynamic_index_in_dim(by_block, rcv_pos, axis=1, keepdims=False)
+    col_index = (run_len * run_ids + STRIDE * within + mine).reshape(-1)
+    groups = jnp.arange(src_rows // STRIDE, dtype=jnp.int32)
+    row_index = STRIDE * groups + lax.dynamic_index_in_dim(
+        panel_offset.reshape(src_count, -1), src_pos, axis=0, keepdims=False
+    )
+    return col_index, row_index
+
+
+def record_rims(rec, src_count, rcv_count, rcv_pos):
+    ring = [(i, (i + 1) % rcv_count) for i in range(rcv_count)]
+    back = [(b, a) for a, b in ring]
+    below = lax.ppermute(rec[:, :, :HALO], "rcv", back)
+    above = lax.ppermute(rec[:, :, -HALO:], "rcv", ring)
+    zero = jnp.zeros_like(below[:, :1])
+    below = jnp.where(
+        rcv_pos == rcv_count - 1, jnp.concatenate([below[:, 1:], zero], axis=1), below
+    )
+    above = jnp.where(rcv_pos == 0, jnp.concatenate([zero, above[:, :-1]], axis=1), above)
+    rims = jnp.concatenate([below, above], axis=2)
+    head = jnp.concatenate([rec[..., :HALO], rims[..., :HALO]], axis=2)
+    tail = jnp.concatenate([rec[..., -HALO:], rims[..., -HALO:]], axis=2)
+    line = [(i, i + 1) for i in range(src_count - 1)]
+    after = lax.ppermute(head, "src", [(b, a) for a, b in line])
+    before = lax.ppermute(tail, "src", line)
+    gap = jnp.zeros(after.shape[:-1] + (128 - 2 * HALO,), after.dtype)
+    return rims, jnp.concatenate([after, gap, before], axis=-1)
+
+
+def shards(record, panel_offset):
+    src_count = lax.axis_size("src")
+    rcv_count = lax.axis_size("rcv")
+    freqs, _, rcv_cols, src_rows = record.shape
+    run_len = rcv_cols // src_count
+    if freqs != 1 or run_len % 16 or src_rows % 128:
+        return plain_shards(record, panel_offset)
+    src_pos = lax.axis_index("src")
+    rcv_pos = lax.axis_index("rcv")
+    panel = panel_offset.shape[0]
+    col_index, row_index = panel_places(
+        panel_offset, src_count, rcv_count, src_pos, rcv_pos, run_len, src_rows
+    )
+    rec = record[0]
+    col_pick = (jnp.arange(rcv_cols)[:, None] == col_index[None, :]).astype(record.dtype)
+    row_pick = (jnp.arange(src_rows)[:, None] == row_index[None, :]).astype(record.dtype)
+    front = lax.dot_general(
+        rec, col_pick, (((1,), (0,)), ((), ())), preferred_element_type=jnp.float32
+    ).astype(record.dtype)
+    behind = lax.dot_general(
+        rec, row_pick, (((2,), (0,)), ((), ())), preferred_element_type=jnp.float32
+    ).astype(record.dtype)
+    front = lax.all_to_all(
+        front.reshape(2, rcv_count, run_len, -1), "rcv", split_axis=1, concat_axis=1, tiled=True
+    )
+    behind = lax.all_to_all(
+        behind.reshape(2, src_count, run_len, -1), "src", split_axis=1, concat_axis=1, tiled=True
+    )
+    own = average_call(front, behind, panel)
+    total = src_count * rcv_count
+    line = [(i, i + 1) for i in range(total - 1)]
+    below = lax.ppermute(own[:, :HALO], ("src", "rcv"), [(b, a) for a, b in line])
+    above = lax.ppermute(own[:, -HALO:], ("src", "rcv"), line)
+    own = jnp.concatenate([own, below, above], axis=1)
+    right = lax.all_gather(own, "src", axis=0)
+    left = lax.all_gather(own, "rcv", axis=0)
+    rims, sides = record_rims(
+        rec.reshape(2, src_count, run_len, src_rows), src_count, rcv_count, rcv_pos
+    )
+    return sweep_call(record, rims, sides, right, left)
+
 
 def solution(mesh):
     in_specs = (P(None, None, "rcv", "src"), P())

time: 656 us -> 231 us (0.35); the launches traced: 644 us -> 230 us
  other arithmetic: 355 us -> 3.14 us
  local copies, waits for them, and re-layouts: 133 us -> 7.7 us
  Pallas kernels: 0 us -> 52.7 us
  waiting for transfers between devices: 101 us -> 120 us
    convert_element_type x11 -> x0, other arithmetic: 168 us -> none  [the longest x2 109 us: neighbour_sum(): recv_total.astype(jnp.bfloat16)]
    add x3, other arithmetic: 135 us -> 0.09 us  [the longest x2 0.08 us: panel_places(): col_index = (run_len * run_ids + STRIDE * within + mine).reshape(-1)]
    pallas_call x0 -> x2, Pallas kernels: none -> 52.7 us  [the longest x1 50.7 us: sweep_call(): pl.pallas_call(functools.partial(sweep_kernel, panel ** (-0.5)), grid=(ru...]
    another operation x5 -> x0, other arithmetic: 46.7 us -> none
    slice x10 -> x5, local copies, waits for them, and re-layouts: 45 us -> 2.39 us  [the longest x1 1.31 us: record_rims(): head = jnp.concatenate([rec[..., :HALO], rims[..., :HALO]], axis=2)]
    unnamed x44 -> x2, local copies, waits for them, and re-layouts: 34.9 us -> 0.01 us
    concatenate x2 -> x1, local copies, waits for them, and re-layouts: 28.3 us -> 0.08 us  [record_rims(): return (rims, jnp.concatenate([after, gap, before], axis=-1))]
    ppermute x8 -> x6, waiting for transfers between devices: 6.04 us -> 31.1 us  [the longest x1 16.7 us: record_rims(): after = lax.ppermute(head, 'src', [(b, a) for a, b in line])]
  transfers between devices with their start and end apart: 12 -> 10, of which waited for: 6 -> 9; matrix products, arithmetic and copies ran while one was open for 7% -> 5% of each run, Pallas kernels for 0% -> 0%
where the time goes in v1:
time: 231 us; the launch traced here: 230 us
  waiting for transfers between devices  120 us (52%)
  Pallas kernels  52.7 us (23%)
  starting transfers between devices  25.2 us (11%)
  between operations  14.2 us (6%)
  local copies, waits for them, and re-layouts  7.7 us (3%)
  matrix products  7.29 us (3%)
  other arithmetic  3.14 us (1%)
    all_gather x1, waiting for transfers between devices, shards(): left = lax.all_gather(own, 'rcv', axis=0)  54.9 us
    pallas_call x1, Pallas kernels, sweep_call(): pl.pallas_call(functools.partial(sweep_kernel, panel ** (-0.5)), grid=(ru...  50.7 us
    all_to_all x1, waiting for transfers between devices, shards(): lax.all_to_all(front.reshape(2, rcv_count, run_len, -1), 'rcv', split_axi...  20.9 us
    ppermute x1, waiting for transfers between devices, record_rims(): after = lax.ppermute(head, 'src', [(b, a) for a, b in line])  16.7 us
    ppermute x1, waiting for transfers between devices, record_rims(): before = lax.ppermute(tail, 'src', line)  8.1 us
    all_gather x1, waiting for transfers between devices, shards(): right = lax.all_gather(own, 'src', axis=0)  7.55 us
    all_to_all x1, starting transfers between devices, shards(): lax.all_to_all(behind.reshape(2, src_count, run_len, -1), 'src', split_ax...  5.16 us
    all_to_all x1, waiting for transfers between devices, shards(): lax.all_to_all(behind.reshape(2, src_count, run_len, -1), 'src', split_ax...  5.11 us
  transfers between devices with their start and end apart: 10, of which 9 were waited for; matrix products, arithmetic and copies ran while one was open for 5% of the time, Pallas kernels for 0%

profile of v1, /device:TPU:0, one launch (start us, length us, event | category | flops | bytes accessed | tf_op | source)
XLA Modules:
  0.0 230.5 jit_solution(7145067405910109283)
XLA Ops:
  8.0 4.0 %fusion.13 = bf16[2,768,192]{1,2,0:T(8,128)(2,1)S(1)} fusion(bf16[1,2,768,1536]{3,2,1,0:T(8,128)(2,1)} %record_ref.1, s32[192]{0:T(256)S(1)} %bitcast.33), kind=kOutput, calls=%fused_computation.7 | convolution fusion | flops 906559488 | bytes 5309184 | tf_op jit(solution)/shard_map/dot_general | solution.py:444
  12.7 1.3 copy.19
  14.0 5.2 %all-to-all-start.1 = ((bf16[2,4,192,192]{3,2,0,1:T(8,128)(2,1)}), bf16[2,4,192,192]{3,2,0,1:T(8,128)(2,1)S(1)}, u32[]{:S(2)}, u32[]{:S(2)}) async-start(bf16[2,4,192,192]{3,2,0,1:T(8,128)(2,1)} %copy.19), calls=%async_computation.1 | async-start | bytes 1572864 | tf_op jit(solution)/shard_map/all_to_all | solution.py:450
  19.6 3.2 %fusion.7 = bf16[2,1536,96]{1,2,0:T(8,128)(2,1)S(1)} fusion(bf16[1,2,768,1536]{3,2,1,0:T(8,128)(2,1)} %record_ref.1, s32[96]{0:T(128)S(1)} %add.48), kind=kOutput, calls=%fused_computation.5 | convolution fusion | flops 453353472 | bytes 5308800 | tf_op jit(solution)/shard_map/dot_general | solution.py:441
  23.4 1.5 copy.18
  24.9 5.1 %all-to-all-done.1 = bf16[2,4,192,192]{3,2,0,1:T(8,128)(2,1)S(1)} async-done(((bf16[2,4,192,192]{3,2,0,1:T(8,128)(2,1)}), bf16[2,4,192,192]{3,2,0,1:T(8,128)(2,1)S(1)}, u32[]{:S(2)}, u32[]{:S(2)}) %all-to-all-start.1) | async-done | bytes 589856 | tf_op jit(solution)/shard_map/all_to_all | solution.py:450
  30.0 4.9 %all-to-all-start = ((bf16[2,8,192,96]{3,2,0,1:T(8,128)(2,1)}), bf16[2,8,192,96]{3,2,0,1:T(8,128)(2,1)S(1)}, u32[]{:S(2)}, u32[]{:S(2)}) async-start(bf16[2,8,192,96]{3,2,0,1:T(8,128)(2,1)} %copy.18), calls=%async_computation | async-start | bytes 1572864 | tf_op jit(solution)/shard_map/all_to_all | solution.py:447
  35.0 20.9 %all-to-all-done = bf16[2,8,192,96]{3,2,0,1:T(8,128)(2,1)S(1)} async-done(((bf16[2,8,192,96]{3,2,0,1:T(8,128)(2,1)}), bf16[2,8,192,96]{3,2,0,1:T(8,128)(2,1)S(1)}, u32[]{:S(2)}, u32[]{:S(2)}) %all-to-all-start) | async-done | bytes 589856 | tf_op jit(solution)/shard_map/all_to_all | solution.py:447
  56.0 2.0 shard_map.41
  57.9 1.3 collective-permute-start.4
  59.2 3.0 %collective-permute-start.5 = (bf16[2,8,768]{2,1,0:T(8,128)(2,1)S(1)}, bf16[2,8,768]{2,1,0:T(8,128)(2,1)S(1)}, u32[]{:S(2)}, u32[]{:S(2)}) collective-permute-start(bf16[2,8,768]{2,1,0:T(8,128)(2,1)S(1)} %get-tuple-element.7), channel_id=1, source_target_pairs={{0,1},{1,2},{2,3},{3,4},{4,5},{5,6},{6,7},{7,8},{8,9},{9,10},{10,1... | collective-permute-start | bytes 73736 | tf_op jit(solution)/shard_map/ppermute | solution.py:457
  64.8 1.1 fusion.25
  65.8 5.0 %collective-permute-start = (bf16[2,4,8,1536]{3,2,1,0:T(8,128)(2,1)S(1)}, bf16[2,4,8,1536]{3,2,1,0:T(8,128)(2,1)S(1)}, u32[]{:S(2)}, u32[]{:S(2)}) collective-permute-start(bf16[2,4,8,1536]{3,2,1,0:T(8,128)(2,1)S(1)} %get-tuple-element.4), channel_id=1, source_target_pairs={{1,0},{2,1},{3,2},{4,3},{5,4},{6,5},{7,6},{0,7},{9,8},{10,9},{11,1... | collective-permute-start | bytes 589832 | tf_op jit(solution)/shard_map/ppermute | solution.py:408
  70.9 1.3 fusion.24
  72.2 1.8 collective-permute-done
  74.0 3.7 %collective-permute-done.1 = bf16[2,4,8,1536]{3,2,1,0:T(8,128)(2,1)S(1)} collective-permute-done((bf16[2,4,8,1536]{3,2,1,0:T(8,128)(2,1)S(1)}, bf16[2,4,8,1536]{3,2,1,0:T(8,128)(2,1)S(1)}, u32[]{:S(2)}, u32[]{:S(2)}) %collective-permute-start.1) | collective-permute-done | bytes 196640 | tf_op jit(solution)/shard_map/ppermute | solution.py:409
  78.0 4.3 %collective-permute-start.3 = (bf16[2,4,208,8]{3,2,1,0:T(8,128)(2,1)S(1)}, bf16[2,4,208,8]{3,2,1,0:T(8,128)(2,1)S(1)}, u32[]{:S(2)}, u32[]{:S(2)}) collective-permute-start(bf16[2,4,208,8]{3,2,1,0:T(8,128)(2,1)S(1)} %pad_maximum_fusion.3), channel_id=1, source_target_pairs={{0,8},{8,16},{16,24},{1,9},{9,17},{17,25},{2,10},{10,18},{18,26},{... | collective-permute-start | bytes 79880 | tf_op jit(solution)/shard_map/ppermute | solution.py:420
  82.3 1.5 collective-permute-start.2
  84.6 8.1 %collective-permute-done.3 = bf16[2,4,208,8]{3,2,1,0:T(8,128)(2,1)S(1)} collective-permute-done((bf16[2,4,208,8]{3,2,1,0:T(8,128)(2,1)S(1)}, bf16[2,4,208,8]{3,2,1,0:T(8,128)(2,1)S(1)}, u32[]{:S(2)}, u32[]{:S(2)}) %collective-permute-start.3) | collective-permute-done | bytes 26656 | tf_op jit(solution)/shard_map/ppermute | solution.py:420
  92.7 16.7 %collective-permute-done.2 = bf16[2,4,208,8]{3,2,1,0:T(8,128)(2,1)S(1)} collective-permute-done((bf16[2,4,208,8]{3,2,1,0:T(8,128)(2,1)S(1)}, bf16[2,4,208,8]{3,2,1,0:T(8,128)(2,1)S(1)}, u32[]{:S(2)}, u32[]{:S(2)}) %collective-permute-start.2) | collective-permute-done | bytes 26656 | tf_op jit(solution)/shard_map/ppermute | solution.py:419
  109.4 1.0 pad_maximum_fusion.4.side_ref
  110.5 7.6 %all-gather.5.cloned.1.call-done = bf16[8,208,768]{2,1,0:T(8,128)(2,1)} async-done(((bf16[2,208,768]{2,1,0:T(8,128)(2,1)}), bf16[8,208,768]{2,1,0:T(8,128)(2,1)}) %all-gather.5.cloned.1.call-update) | async-done | bytes 2555920 | tf_op jit(solution)/shard_map/all_gather | solution.py:459
  118.0 54.9 %all-gather.7.cloned.1.call-done = bf16[16,208,768]{2,1,0:T(8,128)(2,1)} async-done(((bf16[2,208,768]{2,1,0:T(8,128)(2,1)}), bf16[16,208,768]{2,1,0:T(8,128)(2,1)}) %all-gather.7.cloned.1.call-update) | async-done | bytes 5111824 | tf_op jit(solution)/shard_map/all_gather | solution.py:460
  172.9 50.7 %shard_map.42 = (bf16[1,2,768,1536]{3,2,1,0:T(8,128)(2,1)}, bf16[1,2,768,1536]{3,2,1,0:T(8,128)(2,1)}) custom-call(bf16[1,2,768,1536]{3,2,1,0:T(8,128)(2,1)} %record_ref.1, bf16[2,4,16,1536]{3,2,1,0:T(8,128)(2,1)} %pad_maximum_fusion.1.rim_ref, bf16[2,4,208,128]{3,2,1,0:T(8,128)(2,1)} %pad_maximum_fusion.4.side_ref, bf16[4,2,208,768]{3,2,1,0:T(8,128)(2,1)} %bitcast.35, ...), custom_call_target="tpu_custom_call" | custom-call | flops 20000000000 | bytes 18874368 | tf_op jit(solution)/shard_map/pallas_call | solution.py:325
  (35 shorter events, 6.2 us)
Async XLA Ops:
  7.9 11.3 %copy-start = (s32[768]{0:T(1024)S(1)}, s32[768]{0:T(1024)}, u32[]{:S(2)}) copy-start(s32[768]{0:T(1024)} %param.3) | copy-start | bytes 9220
  14.0 16.0 %all-to-all-start.1 = ((bf16[2,4,192,192]{3,2,0,1:T(8,128)(2,1)}), bf16[2,4,192,192]{3,2,0,1:T(8,128)(2,1)S(1)}, u32[]{:S(2)}, u32[]{:S(2)}) async-start(bf16[2,4,192,192]{3,2,0,1:T(8,128)(2,1)} %copy.19), calls=%async_computation.1 | async-start | bytes 1572864 | tf_op jit(solution)/shard_map/all_to_all | solution.py:450
  30.0 25.9 %all-to-all-start = ((bf16[2,8,192,96]{3,2,0,1:T(8,128)(2,1)}), bf16[2,8,192,96]{3,2,0,1:T(8,128)(2,1)S(1)}, u32[]{:S(2)}, u32[]{:S(2)}) async-start(bf16[2,8,192,96]{3,2,0,1:T(8,128)(2,1)} %copy.18), calls=%async_computation | async-start | bytes 1572864 | tf_op jit(solution)/shard_map/all_to_all | solution.py:447
  34.9 83.1 %all-gather.5.cloned.1.call-start = ((), (), s32[]{:S(2)}) async-start(), calls=%async_computation.2 | async-start | bytes 3194880 | tf_op jit(solution)/shard_map/all_gather | solution.py:459
  57.9 4.3 %collective-permute-start.4 = (bf16[2,8,768]{2,1,0:T(8,128)(2,1)S(1)}, bf16[2,8,768]{2,1,0:T(8,128)(2,1)S(1)}, u32[]{:S(2)}, u32[]{:S(2)}) collective-permute-start(bf16[2,8,768]{2,1,0:T(8,128)(2,1)S(1)} %get-tuple-element.6), channel_id=1, source_target_pairs={{1,0},{2,1},{3,2},{4,3},{5,4},{6,5},{7,6},{8,7},{9,8},{10,9},{11,1... | collective-permute-start | bytes 73736 | tf_op jit(solution)/shard_map/ppermute | solution.py:456
  59.2 3.9 %collective-permute-start.5 = (bf16[2,8,768]{2,1,0:T(8,128)(2,1)S(1)}, bf16[2,8,768]{2,1,0:T(8,128)(2,1)S(1)}, u32[]{:S(2)}, u32[]{:S(2)}) collective-permute-start(bf16[2,8,768]{2,1,0:T(8,128)(2,1)S(1)} %get-tuple-element.7), channel_id=1, source_target_pairs={{0,1},{1,2},{2,3},{3,4},{4,5},{5,6},{6,7},{7,8},{8,9},{9,10},{10,1... | collective-permute-start | bytes 73736 | tf_op jit(solution)/shard_map/ppermute | solution.py:457
  64.0 108.9 %all-gather.7.cloned.1.call-start = ((), (), s32[]{:S(2)}) async-start(), calls=%async_computation.3 | async-start | bytes 5750784 | tf_op jit(solution)/shard_map/all_gather | solution.py:460
  65.8 8.2 %collective-permute-start = (bf16[2,4,8,1536]{3,2,1,0:T(8,128)(2,1)S(1)}, bf16[2,4,8,1536]{3,2,1,0:T(8,128)(2,1)S(1)}, u32[]{:S(2)}, u32[]{:S(2)}) collective-permute-start(bf16[2,4,8,1536]{3,2,1,0:T(8,128)(2,1)S(1)} %get-tuple-element.4), channel_id=1, source_target_pairs={{1,0},{2,1},{3,2},{4,3},{5,4},{6,5},{7,6},{0,7},{9,8},{10,9},{11,1... | collective-permute-start | bytes 589832 | tf_op jit(solution)/shard_map/ppermute | solution.py:408
  70.8 6.9 %collective-permute-start.1 = (bf16[2,4,8,1536]{3,2,1,0:T(8,128)(2,1)S(1)}, bf16[2,4,8,1536]{3,2,1,0:T(8,128)(2,1)S(1)}, u32[]{:S(2)}, u32[]{:S(2)}) collective-permute-start(bf16[2,4,8,1536]{3,2,1,0:T(8,128)(2,1)S(1)} %get-tuple-element.5), channel_id=1, source_target_pairs={{0,1},{1,2},{2,3},{3,4},{4,5},{5,6},{6,7},{7,0},{8,9},{9,10},{10,1... | collective-permute-start | bytes 589832 | tf_op jit(solution)/shard_map/ppermute | solution.py:409
  78.0 14.8 %collective-permute-start.3 = (bf16[2,4,208,8]{3,2,1,0:T(8,128)(2,1)S(1)}, bf16[2,4,208,8]{3,2,1,0:T(8,128)(2,1)S(1)}, u32[]{:S(2)}, u32[]{:S(2)}) collective-permute-start(bf16[2,4,208,8]{3,2,1,0:T(8,128)(2,1)S(1)} %pad_maximum_fusion.3), channel_id=1, source_target_pairs={{0,8},{8,16},{16,24},{1,9},{9,17},{17,25},{2,10},{10,18},{18,26},{... | collective-permute-start | bytes 79880 | tf_op jit(solution)/shard_map/ppermute | solution.py:420
  82.3 27.1 %collective-permute-start.2 = (bf16[2,4,208,8]{3,2,1,0:T(8,128)(2,1)S(1)}, bf16[2,4,208,8]{3,2,1,0:T(8,128)(2,1)S(1)}, u32[]{:S(2)}, u32[]{:S(2)}) collective-permute-start(bf16[2,4,208,8]{3,2,1,0:T(8,128)(2,1)S(1)} %pad_maximum_fusion.2), channel_id=1, source_target_pairs={{8,0},{16,8},{24,16},{9,1},{17,9},{25,17},{10,2},{18,10},{26,18},{... | collective-permute-start | bytes 79880 | tf_op jit(solution)/shard_map/ppermute | solution.py:419
Sparse Core Ops, SparseCore 0:
  64.1 53.8 all-gather.4
  120.2 52.6 all-gather.6

commit v2 on v1

--- a/solution.py
+++ b/solution.py
@@ -164,6 +164,7 @@
     return (primaries, multiples)
 
 HALO = 2 * REACH
+MESH = pl.DeviceIdType.MESH
 
 
 def wide_spans(width):
@@ -353,41 +354,6 @@
     )(record, rims, sides, right, left)
 
 
-def average_kernel(front_ref, behind_ref, own_ref):
-    srcs = behind_ref.shape[1]
-    rcvs = front_ref.shape[1]
-    panel = own_ref.shape[2]
-    each = panel // (srcs * rcvs)
-    f32, bf = jnp.float32, jnp.bfloat16
-
-    for chan in range(2):
-        total = jnp.zeros(own_ref.shape[1:], f32)
-        for rcv in range(rcvs):
-            shape = (srcs * each, panel)
-            index = lax.broadcasted_iota(jnp.int32, shape, 0)
-            column = lax.broadcasted_iota(jnp.int32, shape, 1)
-            aim = index // each * (rcvs * each) + rcv * each + index % each
-            pick = jnp.where(column == aim, 1.0, 0.0).astype(bf)
-            total = total + jnp.dot(front_ref[chan, rcv], pick, preferred_element_type=f32)
-        for src in range(srcs):
-            shape = (rcvs * each, panel)
-            index = lax.broadcasted_iota(jnp.int32, shape, 0)
-            column = lax.broadcasted_iota(jnp.int32, shape, 1)
-            pick = jnp.where(column == index + src * rcvs * each, 1.0, 0.0).astype(bf)
-            total = total + jnp.dot(behind_ref[chan, src], pick, preferred_element_type=f32)
-        own_ref[chan] = (total * 0.5).astype(bf)
-
-
-def average_call(front, behind, panel):
-    return pl.pallas_call(
-        average_kernel,
-        out_shape=jax.ShapeDtypeStruct((2, front.shape[2], panel), jnp.bfloat16),
-        in_specs=[pl.BlockSpec(memory_space=pltpu.VMEM)] * 2,
-        out_specs=pl.BlockSpec(memory_space=pltpu.VMEM),
-        compiler_params=pltpu.CompilerParams(vmem_limit_bytes=32 * 1024 * 1024),
-    )(front, behind)
-
-
 def panel_places(panel_offset, src_count, rcv_count, src_pos, rcv_pos, run_len, src_rows):
     per_run = run_len // STRIDE
     run_ids = jnp.arange(src_count, dtype=jnp.int32)[:, None]
@@ -401,25 +367,346 @@
     )
     return col_index, row_index
 
-
-def record_rims(rec, src_count, rcv_count, rcv_pos):
-    ring = [(i, (i + 1) % rcv_count) for i in range(rcv_count)]
-    back = [(b, a) for a, b in ring]
-    below = lax.ppermute(rec[:, :, :HALO], "rcv", back)
-    above = lax.ppermute(rec[:, :, -HALO:], "rcv", ring)
-    zero = jnp.zeros_like(below[:, :1])
-    below = jnp.where(
-        rcv_pos == rcv_count - 1, jnp.concatenate([below[:, 1:], zero], axis=1), below
-    )
-    above = jnp.where(rcv_pos == 0, jnp.concatenate([zero, above[:, :-1]], axis=1), above)
-    rims = jnp.concatenate([below, above], axis=2)
-    head = jnp.concatenate([rec[..., :HALO], rims[..., :HALO]], axis=2)
-    tail = jnp.concatenate([rec[..., -HALO:], rims[..., -HALO:]], axis=2)
-    line = [(i, i + 1) for i in range(src_count - 1)]
-    after = lax.ppermute(head, "src", [(b, a) for a, b in line])
-    before = lax.ppermute(tail, "src", line)
-    gap = jnp.zeros(after.shape[:-1] + (128 - 2 * HALO,), after.dtype)
-    return rims, jnp.concatenate([after, gap, before], axis=-1)
+def exchange_kernel(
+    sizes, rec, col_pick, row_pick, left, right, rims, sides,
+    front_tx, front_rx, behind_tx, behind_rx, head_tx, head_rx, tail_tx, tail_rx,
+    first_tx, after_rx, last_tx, before_rx, own, next_rx, prev_rx,
+    front_send, front_recv, behind_send, behind_recv, edge_send, edge_recv,
+    right_send, right_recv, line_send, left_recv, pair_send,
+):
+    srcs, rcvs = sizes
+    src = lax.axis_index("src")
+    rcv = lax.axis_index("rcv")
+    f32, bf = jnp.float32, jnp.bfloat16
+    rcv_cols, src_rows = rec.shape[1:]
+    run_len = rcv_cols // srcs
+    rows = run_len + 2 * HALO
+    panel = left.shape[3]
+    each = panel // (srcs * rcvs)
+    spots = rcvs // 2
+    spot, core = rcv // 2, lax.rem(rcv, 2)
+
+    def remote(source, target, send, recv, where):
+        return pltpu.make_async_remote_copy(
+            src_ref=source, dst_ref=target, send_sem=send, recv_sem=recv,
+            device_id=where, device_id_type=MESH,
+        )
+
+    rcv_peers = [lax.rem(rcv + step, rcvs) for step in range(1, rcvs)]
+    src_peers = [lax.rem(src + step, srcs) for step in range(1, srcs)]
+    last_rcv, first_rcv = rcv == rcvs - 1, rcv == 0
+    has_next = jnp.logical_not(jnp.logical_and(last_rcv, src == srcs - 1))
+    has_prev = jnp.logical_not(jnp.logical_and(first_rcv, src == 0))
+    next_dev = (
+        jnp.where(last_rcv, jnp.minimum(src + 1, srcs - 1), src), jnp.where(last_rcv, 0, rcv + 1)
+    )
+    prev_dev = (
+        jnp.where(first_rcv, jnp.maximum(src - 1, 0), src), jnp.where(first_rcv, rcvs - 1, rcv - 1)
+    )
+    far_next = jnp.logical_and(last_rcv, src < srcs - 1)
+    far_prev = jnp.logical_and(first_rcv, src > 0)
+
+    barrier = pltpu.get_barrier_semaphore()
+    for peer in rcv_peers:
+        pl.semaphore_signal(barrier, inc=1, device_id=(src, peer), device_id_type=MESH)
+    for peer in src_peers:
+        pl.semaphore_signal(barrier, inc=1, device_id=(peer, rcv), device_id_type=MESH)
+
+    @pl.when(far_next)
+    def _():
+        pl.semaphore_signal(barrier, inc=1, device_id=next_dev, device_id_type=MESH)
+
+    @pl.when(far_prev)
+    def _():
+        pl.semaphore_signal(barrier, inc=1, device_id=prev_dev, device_id_type=MESH)
+
+    for chan in range(2):
+        for pair in range(srcs // 2):
+            for buffer, start in ((head_tx, 0), (tail_tx, run_len - 16)):
+                tiles = [
+                    rec[chan, run * run_len + start : run * run_len + start + 16].astype(f32)
+                    for run in (2 * pair, 2 * pair + 1)
+                ]
+                part = slice(0, HALO) if start == 0 else slice(16 - HALO, 16)
+                buffer[chan, 16 * pair : 16 * pair + 16] = jnp.concatenate(
+                    [tile[part] for tile in tiles], axis=0
+                ).astype(bf)
+        picked = lax.dot_general(
+            rec[chan], col_pick[...], (((0,), (0,)), ((), ())), preferred_element_type=f32
+        ).astype(bf)
+        for peer in range(rcvs):
+            front_tx[peer, chan] = picked[peer * run_len : (peer + 1) * run_len]
+
+    pl.semaphore_wait(
+        barrier,
+        rcvs - 1 + srcs - 1 + jnp.where(far_next, 1, 0) + jnp.where(far_prev, 1, 0),
+    )
+
+    fronts = []
+    for index, peer in enumerate(rcv_peers):
+        copy = remote(
+            front_tx.at[peer], front_rx.at[rcv], front_send.at[index], front_recv.at[rcv], (src, peer)
+        )
+        copy.start()
+        fronts.append(copy)
+    front_rx[rcv] = front_tx[rcv]
+    heads = remote(
+        head_tx, head_rx, edge_send.at[0], edge_recv.at[0], (src, lax.rem(rcv + rcvs - 1, rcvs))
+    )
+    tails = remote(tail_tx, tail_rx, edge_send.at[1], edge_recv.at[1], (src, lax.rem(rcv + 1, rcvs)))
+    heads.start()
+    tails.start()
+
+    for chan in range(2):
+        picked = jnp.dot(rec[chan], row_pick[...], preferred_element_type=f32).astype(bf)
+        for peer in range(srcs):
+            behind_tx[peer, chan] = picked[peer * run_len : (peer + 1) * run_len]
+    behinds = []
+    for index, peer in enumerate(src_peers):
+        copy = remote(
+            behind_tx.at[peer], behind_rx.at[src], behind_send.at[index], behind_recv.at[src],
+            (peer, rcv),
+        )
+        copy.start()
+        behinds.append(copy)
+    behind_rx[src] = behind_tx[src]
+
+    heads.wait()
+    tails.wait()
+
+    def edge(buffer, chan, run):
+        if run < 0 or run >= srcs:
+            return jnp.zeros((HALO, src_rows), f32)
+        tile = buffer[chan, run // 2 * 16 : run // 2 * 16 + 16].astype(f32)
+        return tile[run % 2 * HALO : run % 2 * HALO + HALO]
+
+    for chan in range(2):
+        for run in range(srcs):
+            below = jnp.where(last_rcv, edge(head_rx, chan, run + 1), edge(head_rx, chan, run))
+            above = jnp.where(first_rcv, edge(tail_rx, chan, run - 1), edge(tail_rx, chan, run))
+            rim = jnp.concatenate([below, above], axis=0).astype(bf)
+            rims[chan, run] = rim
+            main = slice(run * run_len, (run + 1) * run_len)
+            first_tx[chan, run, :run_len] = rec[chan, main, :128]
+            first_tx[chan, run, run_len:] = rim[:, :128]
+            last_tx[chan, run, :run_len] = rec[chan, main, src_rows - 128 :]
+            last_tx[chan, run, run_len:] = rim[:, src_rows - 128 :]
+
+    low = jnp.maximum(src - 1, 0)
+    high = jnp.minimum(src + 1, srcs - 1)
+    firsts = remote(first_tx, after_rx, edge_send.at[2], edge_recv.at[2], (low, rcv))
+    lasts = remote(last_tx, before_rx, edge_send.at[3], edge_recv.at[3], (high, rcv))
+
+    @pl.when(src > 0)
+    def _():
+        firsts.start()
+
+    @pl.when(src < srcs - 1)
+    def _():
+        lasts.start()
+
+    for index, step in enumerate(range(1, rcvs)):
+        peer = lax.rem(rcv + rcvs - step, rcvs)
+        remote(
+            front_tx.at[peer], front_rx.at[peer], front_send.at[index], front_recv.at[peer],
+            (src, peer),
+        ).wait_recv()
+    for index, step in enumerate(range(1, srcs)):
+        peer = lax.rem(src + srcs - step, srcs)
+        remote(
+            behind_tx.at[peer], behind_rx.at[peer], behind_send.at[index], behind_recv.at[peer],
+            (peer, rcv),
+        ).wait_recv()
+
+    for chan in range(2):
+        total = jnp.zeros((run_len, panel), f32)
+        for peer in range(rcvs):
+            shape = (srcs * each, panel)
+            index = lax.broadcasted_iota(jnp.int32, shape, 0)
+            column = lax.broadcasted_iota(jnp.int32, shape, 1)
+            aim = index // each * (rcvs * each) + peer * each + index % each
+            pick = jnp.where(column == aim, 1.0, 0.0).astype(bf)
+            total = total + jnp.dot(front_rx[peer, chan], pick, preferred_element_type=f32)
+        for peer in range(srcs):
+            shape = (rcvs * each, panel)
+            index = lax.broadcasted_iota(jnp.int32, shape, 0)
+            column = lax.broadcasted_iota(jnp.int32, shape, 1)
+            pick = jnp.where(column == index + peer * rcvs * each, 1.0, 0.0).astype(bf)
+            total = total + jnp.dot(behind_rx[peer, chan], pick, preferred_element_type=f32)
+        own[chan, :run_len] = (total * 0.5).astype(bf)
+
+    to_prev = remote(own.at[:, pl.ds(0, 16)], next_rx, edge_send.at[4], edge_recv.at[4], prev_dev)
+    to_next = remote(
+        own.at[:, pl.ds(run_len - 16, 16)], prev_rx, edge_send.at[5], edge_recv.at[5], next_dev
+    )
+
+    @pl.when(has_prev)
+    def _():
+        to_prev.start()
+
+    @pl.when(has_next)
+    def _():
+        to_next.start()
+
+    @pl.when(has_next)
+    def _():
+        to_prev.wait_recv()
+
+    @pl.when(jnp.logical_not(has_next))
+    def _():
+        next_rx[...] = jnp.zeros_like(next_rx)
+
+    @pl.when(has_prev)
+    def _():
+        to_next.wait_recv()
+
+    @pl.when(jnp.logical_not(has_prev))
+    def _():
+        prev_rx[...] = jnp.zeros_like(prev_rx)
+
+    place = lax.broadcasted_iota(jnp.int32, (2, 2 * HALO, panel), 1)
+    own[:, run_len:] = jnp.where(place < HALO, next_rx[...], prev_rx[...])
+
+    def line(owner_spot, source, up, step):
+        owner = 2 * owner_spot + core
+        shift = 2 if up else -2
+        return remote(
+            source, left.at[owner], line_send.at[0 if up else 1, step], left_recv.at[owner],
+            (src, jnp.clip(rcv + shift, 0, rcvs - 1)),
+        )
+
+    def hand(owner, source):
+        return remote(
+            source, left.at[owner], pair_send.at[owner // 2], left_recv.at[owner],
+            (src, rcv + 1 - 2 * core),
+        )
+
+    @pl.when(spot < spots - 1)
+    def _():
+        line(spot, own, True, 0).start()
+
+    @pl.when(spot > 0)
+    def _():
+        line(spot, own, False, 0).start()
+
+    rights = []
+    for index, peer in enumerate(src_peers):
+        copy = remote(own, right.at[src], right_send.at[index], right_recv.at[src], (peer, rcv))
+        copy.start()
+        rights.append(copy)
+    hand(rcv, own).start()
+    left[rcv] = own[...]
+    right[src] = own[...]
+
+    for step in range(1, spots):
+        for up in (True, False):
+            owner_spot = spot - step if up else spot + step
+            arrives = spot >= step if up else spot + step < spots
+            onward = spot < spots - 1 if up else spot > 0
+
+            @pl.when(arrives)
+            def _():
+                owner = 2 * owner_spot + core
+                line(owner_spot, left.at[owner], up, step - 1).wait_recv()
+                if step < spots - 1:
+
+                    @pl.when(onward)
+                    def _():
+                        line(owner_spot, left.at[owner], up, step).start()
+
+                hand(owner, left.at[owner]).start()
+
+    for copy in fronts + behinds:
+        copy.wait_send()
+
+    @pl.when(src > 0)
+    def _():
+        firsts.wait_send()
+        lasts.wait_recv()
+
+    @pl.when(src < srcs - 1)
+    def _():
+        lasts.wait_send()
+        firsts.wait_recv()
+
+    @pl.when(src == 0)
+    def _():
+        before_rx[...] = jnp.zeros_like(before_rx)
+
+    @pl.when(src == srcs - 1)
+    def _():
+        after_rx[...] = jnp.zeros_like(after_rx)
+
+    lane = lax.broadcasted_iota(jnp.int32, (rows, 128), 1)
+    zero = jnp.zeros((rows, 128), bf)
+    for chan in range(2):
+        for run in range(srcs):
+            sides[chan, run] = jnp.where(
+                lane < HALO, after_rx[chan, run], jnp.where(lane >= 128 - HALO, before_rx[chan, run], zero)
+            )
+
+    @pl.when(has_prev)
+    def _():
+        to_prev.wait_send()
+
+    @pl.when(has_next)
+    def _():
+        to_next.wait_send()
+
+    for copy in rights:
+        copy.wait_send()
+    for step in range(1, srcs):
+        peer = lax.rem(src + srcs - step, srcs)
+        remote(own, right.at[peer], right_send.at[0], right_recv.at[peer], (peer, rcv)).wait_recv()
+    for step in range(spots - 1):
+        @pl.when(jnp.logical_and(spot < spots - 1, spot >= step))
+        def _():
+            line(spot, own, True, step).wait_send()
+
+        @pl.when(jnp.logical_and(spot > 0, spot + step < spots))
+        def _():
+            line(spot, own, False, step).wait_send()
+
+    for index in range(spots):
+        hand(2 * index + core, own).wait_send()
+        hand(2 * index + 1 - core, own).wait_recv()
+
+
+def exchange_call(rec, col_pick, row_pick, srcs, rcvs, panel):
+    _, rcv_cols, src_rows = rec.shape
+    run_len = rcv_cols // srcs
+    rows = run_len + 2 * HALO
+    bf = jnp.bfloat16
+    vmem = pl.BlockSpec(memory_space=pltpu.VMEM)
+    front = (rcvs, 2, run_len, col_pick.shape[1])
+    behind = (srcs, 2, run_len, row_pick.shape[1])
+    edges = (2, HALO * srcs, src_rows)
+    side = (2, srcs, rows, 128)
+    shapes = [front, front, behind, behind, edges, edges, edges, edges, side, side, side, side]
+    shapes += [(2, rows, panel), (2, 16, panel), (2, 16, panel)]
+    dma = pltpu.SemaphoreType.DMA
+    return pl.pallas_call(
+        functools.partial(exchange_kernel, (srcs, rcvs)),
+        out_shape=(
+            jax.ShapeDtypeStruct((rcvs, 2, rows, panel), bf),
+            jax.ShapeDtypeStruct((srcs, 2, rows, panel), bf),
+            jax.ShapeDtypeStruct((2, srcs, 2 * HALO, src_rows), bf),
+            jax.ShapeDtypeStruct(side, bf),
+        ),
+        in_specs=[vmem] * 3,
+        out_specs=(vmem,) * 4,
+        scratch_shapes=[pltpu.VMEM(shape, bf) for shape in shapes]
+        + [
+            dma((rcvs,)), dma((rcvs,)), dma((srcs,)), dma((srcs,)), dma((6,)), dma((6,)),
+            dma((srcs,)), dma((srcs,)), dma((2, rcvs // 2)), dma((rcvs,)), dma((rcvs // 2,)),
+        ],
+        compiler_params=pltpu.CompilerParams(
+            collective_id=0, has_side_effects=True, vmem_limit_bytes=48 * 1024 * 1024
+        ),
+        cost_estimate=pl.CostEstimate(
+            flops=2_000_000_000, bytes_accessed=8 * rec.size, transcendentals=0
+        ),
+    )(rec, col_pick, row_pick)
 
 
 def shards(record, panel_offset):
@@ -427,7 +714,7 @@
     rcv_count = lax.axis_size("rcv")
     freqs, _, rcv_cols, src_rows = record.shape
     run_len = rcv_cols // src_count
-    if freqs != 1 or run_len % 16 or src_rows % 128:
+    if freqs != 1 or run_len % 16 or src_rows % 128 or src_count % 2 or rcv_count % 2:
         return plain_shards(record, panel_offset)
     src_pos = lax.axis_index("src")
     rcv_pos = lax.axis_index("rcv")
@@ -438,29 +725,7 @@
     rec = record[0]
     col_pick = (jnp.arange(rcv_cols)[:, None] == col_index[None, :]).astype(record.dtype)
     row_pick = (jnp.arange(src_rows)[:, None] == row_index[None, :]).astype(record.dtype)
-    front = lax.dot_general(
-        rec, col_pick, (((1,), (0,)), ((), ())), preferred_element_type=jnp.float32
-    ).astype(record.dtype)
-    behind = lax.dot_general(
-        rec, row_pick, (((2,), (0,)), ((), ())), preferred_element_type=jnp.float32
-    ).astype(record.dtype)
-    front = lax.all_to_all(
-        front.reshape(2, rcv_count, run_len, -1), "rcv", split_axis=1, concat_axis=1, tiled=True
-    )
-    behind = lax.all_to_all(
-        behind.reshape(2, src_count, run_len, -1), "src", split_axis=1, concat_axis=1, tiled=True
-    )
-    own = average_call(front, behind, panel)
-    total = src_count * rcv_count
-    line = [(i, i + 1) for i in range(total - 1)]
-    below = lax.ppermute(own[:, :HALO], ("src", "rcv"), [(b, a) for a, b in line])
-    above = lax.ppermute(own[:, -HALO:], ("src", "rcv"), line)
-    own = jnp.concatenate([own, below, above], axis=1)
-    right = lax.all_gather(own, "src", axis=0)
-    left = lax.all_gather(own, "rcv", axis=0)
-    rims, sides = record_rims(
-        rec.reshape(2, src_count, run_len, src_rows), src_count, rcv_count, rcv_pos
-    )
+    left, right, rims, sides = exchange_call(rec, col_pick, row_pick, src_count, rcv_count, panel)
     return sweep_call(record, rims, sides, right, left)
 
 

time: 231 us -> 139 us (0.60)
  waiting for transfers between devices: 120 us -> 0 us
  Pallas kernels: 52.7 us -> 132 us
  starting transfers between devices: 25.2 us -> 0 us
  between operations: 14.2 us -> 0.69 us
  matrix products: 7.29 us -> 0 us
  local copies, waits for them, and re-layouts: 7.7 us -> 4.79 us
  other arithmetic: 3.14 us -> 0.51 us
    pallas_call x1, Pallas kernels: 1.98 us -> 81.6 us  [exchange_call(): pl.pallas_call(functools.partial(exchange_kernel, (srcs, rcvs)), out_shap...]
    all_gather x2 -> x0, waiting for transfers between devices: 62.4 us -> none  [the longest x1 54.9 us: shards(): left = lax.all_gather(own, 'rcv', axis=0)]
    ppermute x6 -> x0, waiting for transfers between devices: 31.1 us -> none  [the longest x1 16.7 us: record_rims(): after = lax.ppermute(head, 'src', [(b, a) for a, b in line])]
    all_to_all x2 -> x0, waiting for transfers between devices: 26 us -> none  [the longest x1 20.9 us: shards(): lax.all_to_all(front.reshape(2, rcv_count, run_len, -1), 'rcv', split_axi...]
    ppermute x6 -> x0, starting transfers between devices: 15.1 us -> none  [the longest x1 5.01 us: record_rims(): below = lax.ppermute(rec[:, :, :HALO], 'rcv', back)]
    all_to_all x2 -> x0, starting transfers between devices: 10.1 us -> none  [the longest x1 5.16 us: shards(): lax.all_to_all(behind.reshape(2, src_count, run_len, -1), 'src', split_ax...]
    dot_general x2 -> x0, matrix products: 7.29 us -> none  [the longest x1 4.04 us: shards(): lax.dot_general(rec, row_pick, (((2,), (0,)), ((), ())), preferred_elemen...]
    reshape x4 -> x0, local copies, waits for them, and re-layouts: 4.09 us -> none  [the longest x2 2.09 us: shards(): front.reshape(2, rcv_count, run_len, -1)]
  transfers between devices with their start and end apart: 10 -> 0, of which waited for: 9 -> 0; matrix products, arithmetic and copies ran while one was open for 5% -> 0% of each run, Pallas kernels for 0% -> 0%
where the time goes in v2:
time: 139 us; the launch traced here: 138 us
  Pallas kernels  132 us (95%)
  local copies, waits for them, and re-layouts  4.79 us (3%)
    pallas_call x1, Pallas kernels, exchange_call(): pl.pallas_call(functools.partial(exchange_kernel, (srcs, rcvs)), out_shap...  81.6 us
    pallas_call x1, Pallas kernels, sweep_call(): pl.pallas_call(functools.partial(sweep_kernel, panel ** (-0.5)), grid=(ru...  50.7 us
    unnamed x6, local copies, waits for them, and re-layouts  3.06 us

profile of v2, /device:TPU:0, one launch (start us, length us, event | category | flops | bytes accessed | tf_op | source)
XLA Modules:
  0.0 138.3 jit_solution(11892668417969152039)
XLA Ops:
  0.7 0.1 broadcast_add_fusion
  0.7 0.1 add.42
  0.8 0.8 reshape.47
  1.6 0.8 reshape.46
  2.4 0.1 squeeze.10
  2.5 0.1 fusion.1.col_pick
  2.5 0.4 fusion.row_pick
  2.9 81.6 %shard_map.41 = (bf16[8,2,208,768]{3,2,1,0:T(8,128)(2,1)}, bf16[4,2,208,768]{3,2,1,0:T(8,128)(2,1)S(1)}, bf16[2,4,16,1536]{3,2,1,0:T(8,128)(2,1)S(1)}, bf16[2,4,208,128]{3,2,1,0:T(8,128)(2,1)S(1)}) custom-call(bf16[2,768,1536]{2,1,0:T(8,128)(2,1)} %bitcast.3, bf16[768,96]{1,0:T(8,128)(2,1)S(1)} %fusion.1.col_pick, bf16[1536,192]{1,0:T(8,128)(2,1)S(1)} %fusion.row_pick), custom_call_target="tpu_custom_call" | custom-call | flops 2000000000 | bytes 18874368 | tf_op jit(solution)/shard_map/pallas_call | solution.py:688
  84.5 0.0 copy-start
  84.5 1.5 %copy-done = bf16[4,2,208,768]{3,2,1,0:T(8,128)(2,1)} copy-done((bf16[4,2,208,768]{3,2,1,0:T(8,128)(2,1)}, bf16[4,2,208,768]{3,2,1,0:T(8,128)(2,1)S(1)}, u32[]{:S(2)}) %copy-start) | copy-done | bytes 2555928
  86.1 0.0 copy-start.1
  86.1 0.8 copy-done.1
  86.8 0.0 copy-start.2
  86.8 0.8 copy-done.2
  87.6 50.7 %shard_map.42 = (bf16[1,2,768,1536]{3,2,1,0:T(8,128)(2,1)}, bf16[1,2,768,1536]{3,2,1,0:T(8,128)(2,1)}) custom-call(bf16[1,2,768,1536]{3,2,1,0:T(8,128)(2,1)} %record_ref.1, bf16[2,4,16,1536]{3,2,1,0:T(8,128)(2,1)} %copy-done.2, bf16[2,4,208,128]{3,2,1,0:T(8,128)(2,1)} %copy-done.1, bf16[4,2,208,768]{3,2,1,0:T(8,128)(2,1)} %copy-done, ...), custom_call_target="tpu_custom_call" | custom-call | flops 20000000000 | bytes 18874368 | tf_op jit(solution)/shard_map/pallas_call | solution.py:326
  (5 shorter events, 0.1 us)
Async XLA Ops:
  84.5 1.5 %copy-start = (bf16[4,2,208,768]{3,2,1,0:T(8,128)(2,1)}, bf16[4,2,208,768]{3,2,1,0:T(8,128)(2,1)S(1)}, u32[]{:S(2)}) copy-start(bf16[4,2,208,768]{3,2,1,0:T(8,128)(2,1)S(1)} %get-tuple-element.8.right_ref) | copy-start | bytes 7667716
  86.1 0.8 copy-start.1
  86.8 0.8 copy-start.2

commit v3 on v2

--- a/solution.py
+++ b/solution.py
@@ -183,52 +183,24 @@
 
 
 def sweep_kernel(
-    scale, record_ref, rim_ref, side_ref, right_ref, left_ref, prim_ref, mult_ref,
-    left_all, right_all, data, pred32, predb, terms, partial, totals, row_band, lane_band
+    scale, record_ref, rim_ref, side_ref, pred_ref, prim_ref, mult_ref,
+    data, predb, terms, partial, totals, row_band, lane_band
 ):
     runs_len = record_ref.shape[2]
     src_rows = record_ref.shape[3]
-    owners = left_ref.shape[0]
     rows = runs_len + 2 * HALO
     width = src_rows + 128
-    panel = left_ref.shape[3]
     f32, bf = jnp.float32, jnp.bfloat16
 
     @pl.when(pl.program_id(0) == 0)
     def _():
         row_band[...] = band((rows, rows), 0, rows)
         lane_band[...] = band((512, 256), 128, 0)
-        left_all[src_rows:, :] = jnp.zeros((128, 2 * panel), bf)
-        for chan in range(2):
-            lanes = slice(chan * panel, (chan + 1) * panel)
-            for owner in range(owners):
-                left_all[owner * runs_len : (owner + 1) * runs_len, lanes] = left_ref[
-                    owner, chan, :runs_len
-                ]
-            after = left_ref[owners - 1, chan, runs_len:]
-            before = left_ref[0, chan, runs_len:]
-            spot = lax.broadcasted_iota(jnp.int32, after.shape, 0)
-            zero = jnp.zeros_like(after)
-            left_all[src_rows : src_rows + 2 * HALO, lanes] = jnp.where(spot < HALO, after, zero)
-            left_all[width - 2 * HALO : width, lanes] = jnp.where(spot >= HALO, before, zero)
 
     for chan in range(2):
         data[chan, :runs_len, :src_rows] = record_ref[0, chan]
         data[chan, runs_len:, :src_rows] = rim_ref[chan, 0]
         data[chan, :, src_rows:] = side_ref[chan, 0]
-    right_real = right_ref[0, 0]
-    right_imag = right_ref[0, 1]
-    right_all[:rows, :panel] = right_real
-    right_all[:rows, panel:] = -right_imag
-    right_all[rows:, :panel] = right_imag
-    right_all[rows:, panel:] = right_real
-    for start, size in wide_spans(width):
-        pred32[:, start : start + size] = lax.dot_general(
-            right_all[...],
-            left_all[start : start + size, :],
-            (((1,), (1,)), ((), ())),
-            preferred_element_type=f32,
-        )
 
     def put_terms(at, lanes, err, here, guess):
         weight = 1.5 - jnp.tanh(err[0] * err[0] + err[1] * err[1])
@@ -271,13 +243,12 @@
     @pl.loop(0, rows // 16)
     def _(step):
         at = pl.ds(pl.multiple_of(step * 16, 16), 16)
-        at_imag = pl.ds(pl.multiple_of(rows + step * 16, 16), 16)
         for block in range(width // 128):
             lanes = slice(block * 128, (block + 1) * 128)
             here = [data[chan, at, lanes].astype(f32) for chan in range(2)]
             guess = []
-            for chan, spot in enumerate((at, at_imag)):
-                rounded = pred32[spot, lanes].astype(bf)
+            for chan in range(2):
+                rounded = pred_ref[0, chan, at, lanes].astype(bf)
                 predb[chan, at, lanes] = rounded
                 guess.append(rounded.astype(f32))
             put_terms(at, lanes, here, here, guess)
@@ -285,11 +256,10 @@
     @pl.loop(0, runs_len // 16)
     def _(step):
         at = pl.ds(pl.multiple_of(step * 16, 16), 16)
-        at_imag = pl.ds(pl.multiple_of(rows + step * 16, 16), 16)
         for block in range(src_rows // 128):
             lanes = slice(block * 128, (block + 1) * 128)
-            mult_ref[0, 0, at, lanes] = (pred32[at, lanes] * scale).astype(bf)
-            mult_ref[0, 1, at, lanes] = (pred32[at_imag, lanes] * scale).astype(bf)
+            for chan in range(2):
+                mult_ref[0, chan, at, lanes] = (pred_ref[0, chan, at, lanes] * scale).astype(bf)
 
     for sweep_step in range(SWEEPS - 1):
         box()
@@ -313,13 +283,10 @@
             prim_ref[0, 1, at, lanes] = err[1].astype(bf)
 
 
-def sweep_call(record, rims, sides, right, left):
+def sweep_call(record, rims, sides, pred, panel):
     _, _, rcv_cols, src_rows = record.shape
-    runs = right.shape[0]
+    runs, _, rows, width = pred.shape
     run_len = rcv_cols // runs
-    rows = run_len + 2 * HALO
-    width = src_rows + 128
-    panel = left.shape[3]
     f32, bf = jnp.float32, jnp.bfloat16
     out = jax.ShapeDtypeStruct(record.shape, bf)
     tile = pl.BlockSpec((1, 2, run_len, src_rows), lambda r: (0, 0, r, 0))
@@ -331,15 +298,11 @@
             tile,
             pl.BlockSpec((2, 1, 2 * HALO, src_rows), lambda r: (0, r, 0, 0)),
             pl.BlockSpec((2, 1, rows, 128), lambda r: (0, r, 0, 0)),
-            pl.BlockSpec((1, 2, rows, panel), lambda r: (r, 0, 0, 0)),
-            pl.BlockSpec(left.shape, lambda r: (0, 0, 0, 0), pipeline_mode=pl.Buffered(1)),
+            pl.BlockSpec((1, 2, rows, width), lambda r: (r, 0, 0, 0)),
         ],
         out_specs=(tile, tile),
         scratch_shapes=[
-            pltpu.VMEM((width, 2 * panel), bf),
-            pltpu.VMEM((2 * rows, 2 * panel), bf),
             pltpu.VMEM((2, rows, width), bf),
-            pltpu.VMEM((2 * rows, width), f32),
             pltpu.VMEM((2, rows, width), bf),
             pltpu.VMEM((3, rows, width), bf),
             pltpu.VMEM((3, rows, width + 256), bf),
@@ -349,30 +312,31 @@
         ],
         compiler_params=pltpu.CompilerParams(vmem_limit_bytes=56 * 1024 * 1024),
         cost_estimate=pl.CostEstimate(
-            flops=20_000_000_000, bytes_accessed=4 * record.size * 2, transcendentals=2 * record.size
+            flops=12_000_000_000, bytes_accessed=4 * record.size * 2, transcendentals=2 * record.size
         ),
-    )(record, rims, sides, right, left)
+    )(record, rims, sides, pred)
 
 
 def panel_places(panel_offset, src_count, rcv_count, src_pos, rcv_pos, run_len, src_rows):
     per_run = run_len // STRIDE
     run_ids = jnp.arange(src_count, dtype=jnp.int32)[:, None]
     within = jnp.arange(per_run, dtype=jnp.int32)[None, :]
-    by_block = panel_offset.reshape(src_count, rcv_count, per_run)
-    mine = lax.dynamic_index_in_dim(by_block, rcv_pos, axis=1, keepdims=False)
-    col_index = (run_len * run_ids + STRIDE * within + mine).reshape(-1)
-    groups = jnp.arange(src_rows // STRIDE, dtype=jnp.int32)
-    row_index = STRIDE * groups + lax.dynamic_index_in_dim(
-        panel_offset.reshape(src_count, -1), src_pos, axis=0, keepdims=False
-    )
+    per_src = src_rows // STRIDE
+    mine = [
+        lax.dynamic_slice(panel_offset, (per_src * run + per_run * rcv_pos,), (per_run,))
+        for run in range(src_count)
+    ]
+    col_index = (run_len * run_ids + STRIDE * within).reshape(-1) + jnp.concatenate(mine)
+    groups = jnp.arange(per_src, dtype=jnp.int32)
+    row_index = STRIDE * groups + lax.dynamic_slice(panel_offset, (per_src * src_pos,), (per_src,))
     return col_index, row_index
 
 def exchange_kernel(
-    sizes, rec, col_pick, row_pick, left, right, rims, sides,
+    sizes, rec, col_pick, row_pick, pred, rims, sides,
     front_tx, front_rx, behind_tx, behind_rx, head_tx, head_rx, tail_tx, tail_rx,
-    first_tx, after_rx, last_tx, before_rx, own, next_rx, prev_rx,
+    first_tx, after_rx, last_tx, before_rx, own, next_rx, prev_rx, picks, left, right, tiles,
     front_send, front_recv, behind_send, behind_recv, edge_send, edge_recv,
-    right_send, right_recv, line_send, left_recv, pair_send,
+    right_send, right_recv, line_send, left_recv, pair_send, rim_send, rim_recv, out_sem,
 ):
     srcs, rcvs = sizes
     src = lax.axis_index("src")
@@ -381,7 +345,8 @@
     rcv_cols, src_rows = rec.shape[1:]
     run_len = rcv_cols // srcs
     rows = run_len + 2 * HALO
-    panel = left.shape[3]
+    width = src_rows + 128
+    panel = right.shape[3]
     each = panel // (srcs * rcvs)
     spots = rcvs // 2
     spot, core = rcv // 2, lax.rem(rcv, 2)
@@ -406,6 +371,7 @@
     far_next = jnp.logical_and(last_rcv, src < srcs - 1)
     far_prev = jnp.logical_and(first_rcv, src > 0)
 
+    left[src_rows:] = jnp.zeros((128, 2 * panel), bf)
     barrier = pltpu.get_barrier_semaphore()
     for peer in rcv_peers:
         pl.semaphore_signal(barrier, inc=1, device_id=(src, peer), device_id_type=MESH)
@@ -423,53 +389,60 @@
     for chan in range(2):
         for pair in range(srcs // 2):
             for buffer, start in ((head_tx, 0), (tail_tx, run_len - 16)):
-                tiles = [
+                ends = [
                     rec[chan, run * run_len + start : run * run_len + start + 16].astype(f32)
                     for run in (2 * pair, 2 * pair + 1)
                 ]
                 part = slice(0, HALO) if start == 0 else slice(16 - HALO, 16)
                 buffer[chan, 16 * pair : 16 * pair + 16] = jnp.concatenate(
-                    [tile[part] for tile in tiles], axis=0
+                    [end[part] for end in ends], axis=0
                 ).astype(bf)
+
+    pl.semaphore_wait(
+        barrier,
+        rcvs - 1 + srcs - 1 + jnp.where(far_next, 1, 0) + jnp.where(far_prev, 1, 0),
+    )
+    heads = remote(
+        head_tx, head_rx, edge_send.at[0], edge_recv.at[0], (src, lax.rem(rcv + rcvs - 1, rcvs))
+    )
+    tails = remote(tail_tx, tail_rx, edge_send.at[1], edge_recv.at[1], (src, lax.rem(rcv + 1, rcvs)))
+    heads.start()
+    tails.start()
+
+    fronts, behinds = [], []
+    for chan in range(2):
         picked = lax.dot_general(
             rec[chan], col_pick[...], (((0,), (0,)), ((), ())), preferred_element_type=f32
         ).astype(bf)
         for peer in range(rcvs):
             front_tx[peer, chan] = picked[peer * run_len : (peer + 1) * run_len]
-
-    pl.semaphore_wait(
-        barrier,
-        rcvs - 1 + srcs - 1 + jnp.where(far_next, 1, 0) + jnp.where(far_prev, 1, 0),
-    )
-
-    fronts = []
-    for index, peer in enumerate(rcv_peers):
-        copy = remote(
-            front_tx.at[peer], front_rx.at[rcv], front_send.at[index], front_recv.at[rcv], (src, peer)
-        )
-        copy.start()
-        fronts.append(copy)
-    front_rx[rcv] = front_tx[rcv]
-    heads = remote(
-        head_tx, head_rx, edge_send.at[0], edge_recv.at[0], (src, lax.rem(rcv + rcvs - 1, rcvs))
-    )
-    tails = remote(tail_tx, tail_rx, edge_send.at[1], edge_recv.at[1], (src, lax.rem(rcv + 1, rcvs)))
-    heads.start()
-    tails.start()
-
+        for index, peer in enumerate(rcv_peers):
+            copy = remote(
+                front_tx.at[peer, chan], front_rx.at[rcv, chan], front_send.at[chan, index],
+                front_recv.at[chan, rcv], (src, peer),
+            )
+            copy.start()
+            fronts.append(copy)
+        front_rx[rcv, chan] = front_tx[rcv, chan]
     for chan in range(2):
         picked = jnp.dot(rec[chan], row_pick[...], preferred_element_type=f32).astype(bf)
         for peer in range(srcs):
             behind_tx[peer, chan] = picked[peer * run_len : (peer + 1) * run_len]
-    behinds = []
-    for index, peer in enumerate(src_peers):
-        copy = remote(
-            behind_tx.at[peer], behind_rx.at[src], behind_send.at[index], behind_recv.at[src],
-            (peer, rcv),
-        )
-        copy.start()
-        behinds.append(copy)
-    behind_rx[src] = behind_tx[src]
+        for index, peer in enumerate(src_peers):
+            copy = remote(
+                behind_tx.at[peer, chan], behind_rx.at[src, chan], behind_send.at[chan, index],
+                behind_recv.at[chan, src], (peer, rcv),
+            )
+            copy.start()
+            behinds.append(copy)
+        behind_rx[src, chan] = behind_tx[src, chan]
+
+    keys = srcs * each
+    for peer in range(rcvs):
+        index = lax.broadcasted_iota(jnp.int32, (keys, panel), 0)
+        column = lax.broadcasted_iota(jnp.int32, (keys, panel), 1)
+        aim = index // each * (rcvs * each) + peer * each + index % each
+        picks[peer * keys : (peer + 1) * keys] = jnp.where(column == aim, 1.0, 0.0).astype(bf)
 
     heads.wait()
     tails.wait()
@@ -505,28 +478,45 @@
     def _():
         lasts.start()
 
-    for index, step in enumerate(range(1, rcvs)):
-        peer = lax.rem(rcv + rcvs - step, rcvs)
-        remote(
-            front_tx.at[peer], front_rx.at[peer], front_send.at[index], front_recv.at[peer],
-            (src, peer),
-        ).wait_recv()
-    for index, step in enumerate(range(1, srcs)):
-        peer = lax.rem(src + srcs - step, srcs)
-        remote(
-            behind_tx.at[peer], behind_rx.at[peer], behind_send.at[index], behind_recv.at[peer],
-            (peer, rcv),
-        ).wait_recv()
-
+    def line(owner_spot, source, up, step, chan):
+        owner = 2 * owner_spot + core
+        shift = 2 if up else -2
+        return remote(
+            source, shard(owner, chan), line_send.at[chan, 0 if up else 1, step],
+            left_recv.at[chan, owner], (src, jnp.clip(rcv + shift, 0, rcvs - 1)),
+        )
+
+    def hand(owner, source, chan):
+        return remote(
+            source, shard(owner, chan), pair_send.at[chan, owner // 2], left_recv.at[chan, owner],
+            (src, rcv + 1 - 2 * core),
+        )
+
+    def shard(owner, chan):
+        return left.at[
+            pl.ds(pl.multiple_of(owner * run_len, 16), run_len), pl.ds(chan * panel, panel)
+        ]
+
+    to_prev, to_next = [], []
     for chan in range(2):
+        for index, step in enumerate(range(1, rcvs)):
+            peer = lax.rem(rcv + rcvs - step, rcvs)
+            remote(
+                front_tx.at[peer, chan], front_rx.at[peer, chan], front_send.at[chan, index],
+                front_recv.at[chan, peer], (src, peer),
+            ).wait_recv()
+        for index, step in enumerate(range(1, srcs)):
+            peer = lax.rem(src + srcs - step, srcs)
+            remote(
+                behind_tx.at[peer, chan], behind_rx.at[peer, chan], behind_send.at[chan, index],
+                behind_recv.at[chan, peer], (peer, rcv),
+            ).wait_recv()
         total = jnp.zeros((run_len, panel), f32)
         for peer in range(rcvs):
-            shape = (srcs * each, panel)
-            index = lax.broadcasted_iota(jnp.int32, shape, 0)
-            column = lax.broadcasted_iota(jnp.int32, shape, 1)
-            aim = index // each * (rcvs * each) + peer * each + index % each
-            pick = jnp.where(column == aim, 1.0, 0.0).astype(bf)
-            total = total + jnp.dot(front_rx[peer, chan], pick, preferred_element_type=f32)
+            total = total + jnp.dot(
+                front_rx[peer, chan], picks[peer * keys : (peer + 1) * keys],
+                preferred_element_type=f32,
+            )
         for peer in range(srcs):
             shape = (rcvs * each, panel)
             index = lax.broadcasted_iota(jnp.int32, shape, 0)
@@ -534,31 +524,55 @@
             pick = jnp.where(column == index + peer * rcvs * each, 1.0, 0.0).astype(bf)
             total = total + jnp.dot(behind_rx[peer, chan], pick, preferred_element_type=f32)
         own[chan, :run_len] = (total * 0.5).astype(bf)
-
-    to_prev = remote(own.at[:, pl.ds(0, 16)], next_rx, edge_send.at[4], edge_recv.at[4], prev_dev)
-    to_next = remote(
-        own.at[:, pl.ds(run_len - 16, 16)], prev_rx, edge_send.at[5], edge_recv.at[5], next_dev
-    )
+        mine = own.at[chan, pl.ds(0, run_len)]
+
+        @pl.when(spot < spots - 1)
+        def _():
+            line(spot, mine, True, 0, chan).start()
+
+        @pl.when(spot > 0)
+        def _():
+            line(spot, mine, False, 0, chan).start()
+
+        hand(rcv, mine, chan).start()
+        to_prev.append(
+            remote(
+                own.at[chan, pl.ds(0, 16)], next_rx.at[chan], edge_send.at[4 + chan],
+                edge_recv.at[4 + chan], prev_dev,
+            )
+        )
+        to_next.append(
+            remote(
+                own.at[chan, pl.ds(run_len - 16, 16)], prev_rx.at[chan], edge_send.at[6 + chan],
+                edge_recv.at[6 + chan], next_dev,
+            )
+        )
+
+        @pl.when(has_prev)
+        def _():
+            to_prev[chan].start()
+
+        @pl.when(has_next)
+        def _():
+            to_next[chan].start()
+
+        left[
+            pl.ds(pl.multiple_of(rcv * run_len, 16), run_len), chan * panel : (chan + 1) * panel
+        ] = own[chan, :run_len]
+
+    @pl.when(has_next)
+    def _():
+        for chan in range(2):
+            to_prev[chan].wait_recv()
+
+    @pl.when(jnp.logical_not(has_next))
+    def _():
+        next_rx[...] = jnp.zeros_like(next_rx)
 
     @pl.when(has_prev)
     def _():
-        to_prev.start()
-
-    @pl.when(has_next)
-    def _():
-        to_next.start()
-
-    @pl.when(has_next)
-    def _():
-        to_prev.wait_recv()
-
-    @pl.when(jnp.logical_not(has_next))
-    def _():
-        next_rx[...] = jnp.zeros_like(next_rx)
-
-    @pl.when(has_prev)
-    def _():
-        to_next.wait_recv()
+        for chan in range(2):
+            to_next[chan].wait_recv()
 
     @pl.when(jnp.logical_not(has_prev))
     def _():
@@ -566,55 +580,115 @@
 
     place = lax.broadcasted_iota(jnp.int32, (2, 2 * HALO, panel), 1)
     own[:, run_len:] = jnp.where(place < HALO, next_rx[...], prev_rx[...])
-
-    def line(owner_spot, source, up, step):
-        owner = 2 * owner_spot + core
-        shift = 2 if up else -2
-        return remote(
-            source, left.at[owner], line_send.at[0 if up else 1, step], left_recv.at[owner],
-            (src, jnp.clip(rcv + shift, 0, rcvs - 1)),
-        )
-
-    def hand(owner, source):
-        return remote(
-            source, left.at[owner], pair_send.at[owner // 2], left_recv.at[owner],
-            (src, rcv + 1 - 2 * core),
-        )
-
-    @pl.when(spot < spots - 1)
-    def _():
-        line(spot, own, True, 0).start()
-
-    @pl.when(spot > 0)
-    def _():
-        line(spot, own, False, 0).start()
-
     rights = []
     for index, peer in enumerate(src_peers):
         copy = remote(own, right.at[src], right_send.at[index], right_recv.at[src], (peer, rcv))
         copy.start()
         rights.append(copy)
-    hand(rcv, own).start()
-    left[rcv] = own[...]
     right[src] = own[...]
 
+    def rim_copy(start, chan, index, which, peer):
+        return remote(
+            own.at[chan, pl.ds(run_len, 2 * HALO)],
+            left.at[pl.ds(start, 2 * HALO), pl.ds(chan * panel, panel)],
+            rim_send.at[chan, index], rim_recv.at[chan, which], (src, peer),
+        )
+
+    rim_ends = ((first_rcv, width - 2 * HALO, 0), (last_rcv, src_rows, 1))
+    for holds, start, which in rim_ends:
+
+        @pl.when(holds)
+        def _():
+            for chan in range(2):
+                for index, peer in enumerate(rcv_peers):
+                    rim_copy(start, chan, index, which, peer).start()
+                left[start : start + 2 * HALO, chan * panel : (chan + 1) * panel] = own[
+                    chan, run_len:
+                ]
+
+    def multiply(start, size):
+        @pl.loop(0, srcs)
+        def _(run):
+            at = pl.ds(start, size)
+            left_real = left[at, :panel]
+            left_imag = left[at, panel:]
+            contract = (((1,), (1,)), ((), ()))
+
+            def dot(one, two):
+                return lax.dot_general(one, two, contract, preferred_element_type=f32)
+
+            right_real = right[run, 0]
+            right_imag = right[run, 1]
+            tiles[run, 0, :, at] = dot(right_real, left_real) - dot(right_imag, left_imag)
+            tiles[run, 1, :, at] = dot(right_real, left_imag) + dot(right_imag, left_real)
+
+    def out_copy(start, size, index):
+        return pltpu.make_async_copy(
+            tiles.at[:, :, :, pl.ds(start, size)],
+            pred.at[:, :, :, pl.ds(start, size)],
+            out_sem.at[index],
+        )
+
+    span = 2 * run_len
+
+    def tile_of(owner_spot):
+        for chan in range(2):
+            hand(2 * owner_spot + 1 - core, shard(rcv, chan), chan).wait_recv()
+        start = pl.multiple_of(owner_spot * span, 128)
+        multiply(start, span)
+        out_copy(start, span, owner_spot).start()
+
+    def tiles_at(step):
+        if step == 0:
+            tile_of(spot)
+            return
+
+        @pl.when(spot >= step)
+        def _():
+            tile_of(spot - step)
+
+        @pl.when(spot + step < spots)
+        def _():
+            tile_of(spot + step)
+
     for step in range(1, spots):
-        for up in (True, False):
-            owner_spot = spot - step if up else spot + step
-            arrives = spot >= step if up else spot + step < spots
-            onward = spot < spots - 1 if up else spot > 0
-
-            @pl.when(arrives)
-            def _():
-                owner = 2 * owner_spot + core
-                line(owner_spot, left.at[owner], up, step - 1).wait_recv()
-                if step < spots - 1:
-
-                    @pl.when(onward)
-                    def _():
-                        line(owner_spot, left.at[owner], up, step).start()
-
-                hand(owner, left.at[owner]).start()
+        if step == spots - 1:
+            for other in range(1, srcs):
+                peer = lax.rem(src + srcs - other, srcs)
+                remote(
+                    own, right.at[peer], right_send.at[0], right_recv.at[peer], (peer, rcv)
+                ).wait_recv()
+            for done in range(spots - 1):
+                tiles_at(done)
+        for chan in range(2):
+            for up in (True, False):
+                owner_spot = spot - step if up else spot + step
+                arrives = spot >= step if up else spot + step < spots
+                onward = spot < spots - 1 if up else spot > 0
+
+                @pl.when(arrives)
+                def _():
+                    owner = 2 * owner_spot + core
+                    block = shard(owner, chan)
+                    line(owner_spot, block, up, step - 1, chan).wait_recv()
+                    if step < spots - 1:
+
+                        @pl.when(onward)
+                        def _():
+                            line(owner_spot, block, up, step, chan).start()
+
+                    hand(owner, block, chan).start()
+
+    for holds, start, which in rim_ends:
+
+        @pl.when(jnp.logical_not(holds))
+        def _():
+            for chan in range(2):
+                rim_copy(start, chan, 0, which, rcv).wait_recv()
+
+    multiply(src_rows, 128)
+    out_copy(src_rows, 128, spots).start()
+    tiles_at(spots - 1)
 
     for copy in fronts + behinds:
         copy.wait_send()
@@ -645,31 +719,42 @@
                 lane < HALO, after_rx[chan, run], jnp.where(lane >= 128 - HALO, before_rx[chan, run], zero)
             )
 
-    @pl.when(has_prev)
-    def _():
-        to_prev.wait_send()
-
-    @pl.when(has_next)
-    def _():
-        to_next.wait_send()
+    for chan in range(2):
+
+        @pl.when(has_prev)
+        def _():
+            to_prev[chan].wait_send()
+
+        @pl.when(has_next)
+        def _():
+            to_next[chan].wait_send()
+
+        for holds, start, which in rim_ends:
+
+            @pl.when(holds)
+            def _():
+                for index, peer in enumerate(rcv_peers):
+                    rim_copy(start, chan, index, which, peer).wait_send()
+
+        mine = own.at[chan, pl.ds(0, run_len)]
+        for step in range(spots - 1):
+
+            @pl.when(jnp.logical_and(spot < spots - 1, spot >= step))
+            def _():
+                line(spot, mine, True, step, chan).wait_send()
+
+            @pl.when(jnp.logical_and(spot > 0, spot + step < spots))
+            def _():
+                line(spot, mine, False, step, chan).wait_send()
+
+        for index in range(spots):
+            hand(2 * index + core, mine, chan).wait_send()
 
     for copy in rights:
         copy.wait_send()
-    for step in range(1, srcs):
-        peer = lax.rem(src + srcs - step, srcs)
-        remote(own, right.at[peer], right_send.at[0], right_recv.at[peer], (peer, rcv)).wait_recv()
-    for step in range(spots - 1):
-        @pl.when(jnp.logical_and(spot < spots - 1, spot >= step))
-        def _():
-            line(spot, own, True, step).wait_send()
-
-        @pl.when(jnp.logical_and(spot > 0, spot + step < spots))
-        def _():
-            line(spot, own, False, step).wait_send()
-
     for index in range(spots):
-        hand(2 * index + core, own).wait_send()
-        hand(2 * index + 1 - core, own).wait_recv()
+        out_copy(index * span, span, index).wait()
+    out_copy(src_rows, 128, spots).wait()
 
 
 def exchange_call(rec, col_pick, row_pick, srcs, rcvs, panel):
@@ -683,28 +768,31 @@
     edges = (2, HALO * srcs, src_rows)
     side = (2, srcs, rows, 128)
     shapes = [front, front, behind, behind, edges, edges, edges, edges, side, side, side, side]
-    shapes += [(2, rows, panel), (2, 16, panel), (2, 16, panel)]
+    shapes += [(2, rows, panel), (2, 16, panel), (2, 16, panel), (panel, panel)]
+    shapes += [(src_rows + 128, 2 * panel), (srcs, 2, rows, panel)]
+    wide = (srcs, 2, rows, src_rows + 128)
     dma = pltpu.SemaphoreType.DMA
     return pl.pallas_call(
         functools.partial(exchange_kernel, (srcs, rcvs)),
         out_shape=(
-            jax.ShapeDtypeStruct((rcvs, 2, rows, panel), bf),
-            jax.ShapeDtypeStruct((srcs, 2, rows, panel), bf),
+            jax.ShapeDtypeStruct(wide, jnp.float32),
             jax.ShapeDtypeStruct((2, srcs, 2 * HALO, src_rows), bf),
             jax.ShapeDtypeStruct(side, bf),
         ),
         in_specs=[vmem] * 3,
-        out_specs=(vmem,) * 4,
+        out_specs=(pl.BlockSpec(memory_space=pl.ANY), vmem, vmem),
         scratch_shapes=[pltpu.VMEM(shape, bf) for shape in shapes]
+        + [pltpu.VMEM(wide, jnp.float32)]
         + [
-            dma((rcvs,)), dma((rcvs,)), dma((srcs,)), dma((srcs,)), dma((6,)), dma((6,)),
-            dma((srcs,)), dma((srcs,)), dma((2, rcvs // 2)), dma((rcvs,)), dma((rcvs // 2,)),
+            dma((2, rcvs)), dma((2, rcvs)), dma((2, srcs)), dma((2, srcs)), dma((8,)), dma((8,)),
+            dma((srcs,)), dma((srcs,)), dma((2, 2, rcvs // 2)), dma((2, rcvs)), dma((2, rcvs // 2)),
+            dma((2, rcvs)), dma((2, 2)), dma((rcvs // 2 + 1,)),
         ],
         compiler_params=pltpu.CompilerParams(
-            collective_id=0, has_side_effects=True, vmem_limit_bytes=48 * 1024 * 1024
+            collective_id=0, has_side_effects=True, vmem_limit_bytes=56 * 1024 * 1024
         ),
         cost_estimate=pl.CostEstimate(
-            flops=2_000_000_000, bytes_accessed=8 * rec.size, transcendentals=0
+            flops=10_000_000_000, bytes_accessed=8 * rec.size, transcendentals=0
         ),
     )(rec, col_pick, row_pick)
 
@@ -714,7 +802,7 @@
     rcv_count = lax.axis_size("rcv")
     freqs, _, rcv_cols, src_rows = record.shape
     run_len = rcv_cols // src_count
-    if freqs != 1 or run_len % 16 or src_rows % 128 or src_count % 2 or rcv_count % 2:
+    if freqs != 1 or run_len % 16 or src_rows % 128 or src_count % 2 or rcv_count % 2 or run_len % 64 or rcv_count < 4:
         return plain_shards(record, panel_offset)
     src_pos = lax.axis_index("src")
     rcv_pos = lax.axis_index("rcv")
@@ -725,8 +813,8 @@
     rec = record[0]
     col_pick = (jnp.arange(rcv_cols)[:, None] == col_index[None, :]).astype(record.dtype)
     row_pick = (jnp.arange(src_rows)[:, None] == row_index[None, :]).astype(record.dtype)
-    left, right, rims, sides = exchange_call(rec, col_pick, row_pick, src_count, rcv_count, panel)
-    return sweep_call(record, rims, sides, right, left)
+    pred, rims, sides = exchange_call(rec, col_pick, row_pick, src_count, rcv_count, panel)
+    return sweep_call(record, rims, sides, pred, panel)
 
 
 def solution(mesh):

time: 139 us -> 136 us (0.978)
  local copies, waits for them, and re-layouts: 4.79 us -> 1.01 us
  other arithmetic: 0.51 us -> 2.89 us
    pallas_call x1, Pallas kernels: 50.7 us -> 37.2 us  [sweep_call(): pl.pallas_call(functools.partial(sweep_kernel, panel ** (-0.5)), grid=(ru...]
    pallas_call x1, Pallas kernels: 81.6 us -> 94.1 us  [exchange_call(): pl.pallas_call(functools.partial(exchange_kernel, (srcs, rcvs)), out_shap...]
    unnamed x6 -> x0, local copies, waits for them, and re-layouts: 3.06 us -> none
    reshape x2 -> x0, local copies, waits for them, and re-layouts: 1.53 us -> none  [the longest x1 0.76 us: panel_places(): panel_offset.reshape(src_count, -1)]
where the time goes in v3:
time: 136 us
  Pallas kernels  131 us (96%)
  other arithmetic  2.89 us (2%)
    pallas_call x1, Pallas kernels, exchange_call(): pl.pallas_call(functools.partial(exchange_kernel, (srcs, rcvs)), out_shap...  94.1 us
    pallas_call x1, Pallas kernels, sweep_call(): pl.pallas_call(functools.partial(sweep_kernel, panel ** (-0.5)), grid=(ru...  37.2 us

profile of v3, /device:TPU:0, one launch (start us, length us, event | category | flops | bytes accessed | tf_op | source)
XLA Modules:
  0.0 135.9 jit_solution(15107665727807809127)
XLA Ops:
  0.6 0.9 fusion.2
  1.6 0.8 dynamic-slice_add_fusion
  2.3 0.1 broadcast_add_fusion
  2.4 0.1 add.58
  2.5 0.1 add_add_fusion
  2.6 0.7 fusion.1.col_pick
  3.3 1.2 fusion.row_pick
  4.5 94.1 %shard_map.41 = (f32[4,2,208,1664]{3,2,1,0:T(8,128)}, bf16[2,4,16,1536]{3,2,1,0:T(8,128)(2,1)}, bf16[2,4,208,128]{3,2,1,0:T(8,128)(2,1)}) custom-call(bf16[2,768,1536]{2,1,0:T(8,128)(2,1)} %bitcast.1, bf16[768,96]{1,0:T(8,128)(2,1)} %fusion.1.col_pick, bf16[1536,192]{1,0:T(8,128)(2,1)} %fusion.row_pick), custom_call_target="tpu_custom_call" | custom-call | flops 10000000000 | bytes 18874368 | tf_op jit(solution)/shard_map/pallas_call | solution.py:775
  98.7 37.2 %shard_map.42 = (bf16[1,2,768,1536]{3,2,1,0:T(8,128)(2,1)}, bf16[1,2,768,1536]{3,2,1,0:T(8,128)(2,1)}) custom-call(bf16[1,2,768,1536]{3,2,1,0:T(8,128)(2,1)} %record_ref.1, bf16[2,4,16,1536]{3,2,1,0:T(8,128)(2,1)} %get-tuple-element.5.rim_ref, bf16[2,4,208,128]{3,2,1,0:T(8,128)(2,1)} %get-tuple-element.6.side_ref, f32[4,2,208,1664]{3,2,1,0:T(8,128)} %get-tuple-element.7.pred_ref), custom_call_target="tpu_custom_call" | custom-call | flops 12000000000 | bytes 18874368 | tf_op jit(solution)/shard_map/pallas_call | solution.py:293
  (2 shorter events, 0.0 us)

commit v4 on v3

--- a/solution.py
+++ b/solution.py
@@ -248,7 +248,7 @@
             here = [data[chan, at, lanes].astype(f32) for chan in range(2)]
             guess = []
             for chan in range(2):
-                rounded = pred_ref[0, chan, at, lanes].astype(bf)
+                rounded = pred_ref[chan, 0, at, lanes].astype(bf)
                 predb[chan, at, lanes] = rounded
                 guess.append(rounded.astype(f32))
             put_terms(at, lanes, here, here, guess)
@@ -259,7 +259,7 @@
         for block in range(src_rows // 128):
             lanes = slice(block * 128, (block + 1) * 128)
             for chan in range(2):
-                mult_ref[0, chan, at, lanes] = (pred_ref[0, chan, at, lanes] * scale).astype(bf)
+                mult_ref[0, chan, at, lanes] = (pred_ref[chan, 0, at, lanes] * scale).astype(bf)
 
     for sweep_step in range(SWEEPS - 1):
         box()
@@ -285,7 +285,7 @@
 
 def sweep_call(record, rims, sides, pred, panel):
     _, _, rcv_cols, src_rows = record.shape
-    runs, _, rows, width = pred.shape
+    _, runs, rows, width = pred.shape
     run_len = rcv_cols // runs
     f32, bf = jnp.float32, jnp.bfloat16
     out = jax.ShapeDtypeStruct(record.shape, bf)
@@ -298,7 +298,7 @@
             tile,
             pl.BlockSpec((2, 1, 2 * HALO, src_rows), lambda r: (0, r, 0, 0)),
             pl.BlockSpec((2, 1, rows, 128), lambda r: (0, r, 0, 0)),
-            pl.BlockSpec((1, 2, rows, width), lambda r: (r, 0, 0, 0)),
+            pl.BlockSpec((2, 1, rows, width), lambda r: (0, r, 0, 0)),
         ],
         out_specs=(tile, tile),
         scratch_shapes=[
@@ -317,24 +317,11 @@
     )(record, rims, sides, pred)
 
 
-def panel_places(panel_offset, src_count, rcv_count, src_pos, rcv_pos, run_len, src_rows):
-    per_run = run_len // STRIDE
-    run_ids = jnp.arange(src_count, dtype=jnp.int32)[:, None]
-    within = jnp.arange(per_run, dtype=jnp.int32)[None, :]
-    per_src = src_rows // STRIDE
-    mine = [
-        lax.dynamic_slice(panel_offset, (per_src * run + per_run * rcv_pos,), (per_run,))
-        for run in range(src_count)
-    ]
-    col_index = (run_len * run_ids + STRIDE * within).reshape(-1) + jnp.concatenate(mine)
-    groups = jnp.arange(per_src, dtype=jnp.int32)
-    row_index = STRIDE * groups + lax.dynamic_slice(panel_offset, (per_src * src_pos,), (per_src,))
-    return col_index, row_index
-
 def exchange_kernel(
-    sizes, rec, col_pick, row_pick, pred, rims, sides,
+    sizes, rec, offset, pred, rims, sides,
     front_tx, front_rx, behind_tx, behind_rx, head_tx, head_rx, tail_tx, tail_rx,
-    first_tx, after_rx, last_tx, before_rx, own, next_rx, prev_rx, picks, left, right, tiles,
+    first_tx, after_rx, last_tx, before_rx, own, next_rx, prev_rx, picks, left, right, right_all, tiles,
+    col_pick, row_pick,
     front_send, front_recv, behind_send, behind_recv, edge_send, edge_recv,
     right_send, right_recv, line_send, left_recv, pair_send, rim_send, rim_recv, out_sem,
 ):
@@ -385,6 +372,25 @@
     @pl.when(far_prev)
     def _():
         pl.semaphore_signal(barrier, inc=1, device_id=prev_dev, device_id_type=MESH)
+
+    offsets = jnp.broadcast_to(offset[...].astype(f32), (8, panel)).astype(bf)
+
+    def pick_from(target, count, group_of, cell_of):
+        groups = lax.broadcasted_iota(jnp.int32, (panel, count), 0)
+        column = lax.broadcasted_iota(jnp.int32, (panel, count), 1)
+        chosen = jnp.where(groups == group_of(column), 1.0, 0.0).astype(bf)
+        mine = jnp.dot(offsets, chosen, preferred_element_type=f32)[:1].astype(jnp.int32)
+        cells = lax.broadcasted_iota(jnp.int32, target.shape, 0)
+        column = lax.broadcasted_iota(jnp.int32, (1, count), 1)
+        target[...] = jnp.where(cells == cell_of(column) + mine, 1.0, 0.0).astype(bf)
+
+    per_src = rcvs * each
+    pick_from(
+        col_pick, srcs * each,
+        lambda j: j // each * per_src + each * rcv + j % each,
+        lambda j: j // each * run_len + STRIDE * (j % each),
+    )
+    pick_from(row_pick, per_src, lambda j: per_src * src + j, lambda j: STRIDE * j)
 
     for chan in range(2):
         for pair in range(srcs // 2):
@@ -606,21 +612,20 @@
                     chan, run_len:
                 ]
 
+    def set_right(run):
+        real, imag = right[run, 0], right[run, 1]
+        top = slice(run * rows, (run + 1) * rows)
+        bottom = slice((srcs + run) * rows, (srcs + run + 1) * rows)
+        right_all[top, :panel] = real
+        right_all[top, panel:] = -imag
+        right_all[bottom, :panel] = imag
+        right_all[bottom, panel:] = real
+
     def multiply(start, size):
-        @pl.loop(0, srcs)
-        def _(run):
-            at = pl.ds(start, size)
-            left_real = left[at, :panel]
-            left_imag = left[at, panel:]
-            contract = (((1,), (1,)), ((), ()))
-
-            def dot(one, two):
-                return lax.dot_general(one, two, contract, preferred_element_type=f32)
-
-            right_real = right[run, 0]
-            right_imag = right[run, 1]
-            tiles[run, 0, :, at] = dot(right_real, left_real) - dot(right_imag, left_imag)
-            tiles[run, 1, :, at] = dot(right_real, left_imag) + dot(right_imag, left_real)
+        at = pl.ds(start, size)
+        tiles[:, :, :, at] = lax.dot_general(
+            right_all[...], left[at, :], (((1,), (1,)), ((), ())), preferred_element_type=f32
+        ).reshape(2, srcs, rows, size)
 
     def out_copy(start, size, index):
         return pltpu.make_async_copy(
@@ -638,18 +643,12 @@
         multiply(start, span)
         out_copy(start, span, owner_spot).start()
 
-    def tiles_at(step):
-        if step == 0:
-            tile_of(spot)
-            return
-
-        @pl.when(spot >= step)
-        def _():
-            tile_of(spot - step)
-
-        @pl.when(spot + step < spots)
-        def _():
-            tile_of(spot + step)
+    def tiles_when(ready):
+        @pl.loop(0, spots)
+        def _(other):
+            @pl.when(ready(jnp.abs(other - spot)))
+            def _():
+                tile_of(other)
 
     for step in range(1, spots):
         if step == spots - 1:
@@ -658,8 +657,9 @@
                 remote(
                     own, right.at[peer], right_send.at[0], right_recv.at[peer], (peer, rcv)
                 ).wait_recv()
-            for done in range(spots - 1):
-                tiles_at(done)
+            for run in range(srcs):
+                set_right(run)
+            tiles_when(lambda gap: gap < spots - 1)
         for chan in range(2):
             for up in (True, False):
                 owner_spot = spot - step if up else spot + step
@@ -688,7 +688,7 @@
 
     multiply(src_rows, 128)
     out_copy(src_rows, 128, spots).start()
-    tiles_at(spots - 1)
+    tiles_when(lambda gap: gap == spots - 1)
 
     for copy in fronts + behinds:
         copy.wait_send()
@@ -757,20 +757,22 @@
     out_copy(src_rows, 128, spots).wait()
 
 
-def exchange_call(rec, col_pick, row_pick, srcs, rcvs, panel):
+def exchange_call(rec, panel_offset, srcs, rcvs):
     _, rcv_cols, src_rows = rec.shape
     run_len = rcv_cols // srcs
     rows = run_len + 2 * HALO
+    panel = panel_offset.shape[0]
+    each = panel // (srcs * rcvs)
     bf = jnp.bfloat16
     vmem = pl.BlockSpec(memory_space=pltpu.VMEM)
-    front = (rcvs, 2, run_len, col_pick.shape[1])
-    behind = (srcs, 2, run_len, row_pick.shape[1])
+    front = (rcvs, 2, run_len, srcs * each)
+    behind = (srcs, 2, run_len, rcvs * each)
     edges = (2, HALO * srcs, src_rows)
     side = (2, srcs, rows, 128)
     shapes = [front, front, behind, behind, edges, edges, edges, edges, side, side, side, side]
     shapes += [(2, rows, panel), (2, 16, panel), (2, 16, panel), (panel, panel)]
-    shapes += [(src_rows + 128, 2 * panel), (srcs, 2, rows, panel)]
-    wide = (srcs, 2, rows, src_rows + 128)
+    shapes += [(src_rows + 128, 2 * panel), (srcs, 2, rows, panel), (2 * srcs * rows, 2 * panel)]
+    wide = (2, srcs, rows, src_rows + 128)
     dma = pltpu.SemaphoreType.DMA
     return pl.pallas_call(
         functools.partial(exchange_kernel, (srcs, rcvs)),
@@ -779,10 +781,14 @@
             jax.ShapeDtypeStruct((2, srcs, 2 * HALO, src_rows), bf),
             jax.ShapeDtypeStruct(side, bf),
         ),
-        in_specs=[vmem] * 3,
+        in_specs=[vmem] * 2,
         out_specs=(pl.BlockSpec(memory_space=pl.ANY), vmem, vmem),
         scratch_shapes=[pltpu.VMEM(shape, bf) for shape in shapes]
-        + [pltpu.VMEM(wide, jnp.float32)]
+        + [
+            pltpu.VMEM(wide, jnp.float32),
+            pltpu.VMEM((rcv_cols, srcs * each), bf),
+            pltpu.VMEM((src_rows, rcvs * each), bf),
+        ]
         + [
             dma((2, rcvs)), dma((2, rcvs)), dma((2, srcs)), dma((2, srcs)), dma((8,)), dma((8,)),
             dma((srcs,)), dma((srcs,)), dma((2, 2, rcvs // 2)), dma((2, rcvs)), dma((2, rcvs // 2)),
@@ -794,7 +800,7 @@
         cost_estimate=pl.CostEstimate(
             flops=10_000_000_000, bytes_accessed=8 * rec.size, transcendentals=0
         ),
-    )(rec, col_pick, row_pick)
+    )(rec, panel_offset.reshape(1, panel))
 
 
 def shards(record, panel_offset):
@@ -804,17 +810,8 @@
     run_len = rcv_cols // src_count
     if freqs != 1 or run_len % 16 or src_rows % 128 or src_count % 2 or rcv_count % 2 or run_len % 64 or rcv_count < 4:
         return plain_shards(record, panel_offset)
-    src_pos = lax.axis_index("src")
-    rcv_pos = lax.axis_index("rcv")
-    panel = panel_offset.shape[0]
-    col_index, row_index = panel_places(
-        panel_offset, src_count, rcv_count, src_pos, rcv_pos, run_len, src_rows
-    )
-    rec = record[0]
-    col_pick = (jnp.arange(rcv_cols)[:, None] == col_index[None, :]).astype(record.dtype)
-    row_pick = (jnp.arange(src_rows)[:, None] == row_index[None, :]).astype(record.dtype)
-    pred, rims, sides = exchange_call(rec, col_pick, row_pick, src_count, rcv_count, panel)
-    return sweep_call(record, rims, sides, pred, panel)
+    pred, rims, sides = exchange_call(record[0], panel_offset, src_count, rcv_count)
+    return sweep_call(record, rims, sides, pred, panel_offset.shape[0])
 
 
 def solution(mesh):

time: 136 us -> 130 us (0.956)
  Pallas kernels: 131 us -> 128 us
  other arithmetic: 2.89 us -> 0 us
    pallas_call x1, Pallas kernels: 94.1 us -> 90.4 us  [exchange_call(): pl.pallas_call(functools.partial(exchange_kernel, (srcs, rcvs)), out_shap...]
    convert_element_type x2 -> x0, other arithmetic: 1.97 us -> none  [the longest x1 1.23 us: shards(): (jnp.arange(src_rows)[:, None] == row_index[None, :]).astype(record.dtype)]
where the time goes in v4:
time: 130 us
  Pallas kernels  128 us (98%)
    pallas_call x1, Pallas kernels, exchange_call(): pl.pallas_call(functools.partial(exchange_kernel, (srcs, rcvs)), out_shap...  90.4 us
    pallas_call x1, Pallas kernels, sweep_call(): pl.pallas_call(functools.partial(sweep_kernel, panel ** (-0.5)), grid=(ru...  37.2 us

profile of v4, /device:TPU:0, one launch (start us, length us, event | category | flops | bytes accessed | tf_op | source)
XLA Modules:
  0.0 129.6 jit_solution(11263919327861295797)
XLA Ops:
  0.6 1.3 reshape.7.offset
  1.9 90.4 %shard_map.41 = (f32[2,4,208,1664]{3,2,1,0:T(8,128)}, bf16[2,4,16,1536]{3,2,1,0:T(8,128)(2,1)}, bf16[2,4,208,128]{3,2,1,0:T(8,128)(2,1)}) custom-call(bf16[2,768,1536]{2,1,0:T(8,128)(2,1)} %bitcast.1, s32[1,768]{1,0:T(1,128)} %reshape.7.offset), custom_call_target="tpu_custom_call" | custom-call | flops 10000000000 | bytes 18874368 | tf_op jit(solution)/shard_map/pallas_call | solution.py:777
  92.3 37.2 %shard_map.42 = (bf16[1,2,768,1536]{3,2,1,0:T(8,128)(2,1)}, bf16[1,2,768,1536]{3,2,1,0:T(8,128)(2,1)}) custom-call(bf16[1,2,768,1536]{3,2,1,0:T(8,128)(2,1)} %record_ref.1, bf16[2,4,16,1536]{3,2,1,0:T(8,128)(2,1)} %get-tuple-element.5.rim_ref, bf16[2,4,208,128]{3,2,1,0:T(8,128)(2,1)} %get-tuple-element.6.side_ref, f32[2,4,208,1664]{3,2,1,0:T(8,128)} %get-tuple-element.7.pred_ref), custom_call_target="tpu_custom_call" | custom-call | flops 12000000000 | bytes 18874368 | tf_op jit(solution)/shard_map/pallas_call | solution.py:293

commit v5 on v4

--- a/solution.py
+++ b/solution.py
@@ -317,11 +317,40 @@
     )(record, rims, sides, pred)
 
 
+def roll(values, shift):
+    return pltpu.roll(values, shift % 128, 1) if shift % 128 else values
+
+
+def lanes_of(values):
+    return lax.broadcasted_iota(jnp.int32, values.shape, 1)
+
+
+def pack_traces(traces):
+    half, quarter = traces.shape[0] // 2, traces.shape[0] // 4
+    wide = jnp.where(
+        lanes_of(traces[:half]) < 64, traces[:half], roll(traces[half:], 64)
+    )
+    lane = lanes_of(traces[:quarter])
+    rest = jnp.zeros((quarter, 128), traces.dtype)
+    for part in range(4):
+        moved = roll(traces[part * quarter : (part + 1) * quarter], 32 * part - 64)
+        rest = jnp.where(lane // 32 == part, moved, rest)
+    return jnp.concatenate([wide, rest], axis=0)
+
+
+def unpack_traces(packed):
+    half = packed.shape[0] * 2 // 3
+    wide = jnp.concatenate([packed[:half], roll(packed[:half], 64)], axis=0)
+    rest = jnp.concatenate([roll(packed[half:], 64 - 32 * part) for part in range(4)], axis=0)
+    lane = lanes_of(wide)
+    return jnp.where(lane < 64, wide, jnp.where(lane < 96, rest, jnp.zeros_like(rest)))
+
+
 def exchange_kernel(
     sizes, rec, offset, pred, rims, sides,
     front_tx, front_rx, behind_tx, behind_rx, head_tx, head_rx, tail_tx, tail_rx,
     first_tx, after_rx, last_tx, before_rx, own, next_rx, prev_rx, picks, left, right, right_all, tiles,
-    col_pick, row_pick,
+    col_pick, row_pick, gathered,
     front_send, front_recv, behind_send, behind_recv, edge_send, edge_recv,
     right_send, right_recv, line_send, left_recv, pair_send, rim_send, rim_recv, out_sem,
 ):
@@ -385,11 +414,19 @@
         target[...] = jnp.where(cells == cell_of(column) + mine, 1.0, 0.0).astype(bf)
 
     per_src = rcvs * each
-    pick_from(
-        col_pick, srcs * each,
-        lambda j: j // each * per_src + each * rcv + j % each,
-        lambda j: j // each * run_len + STRIDE * (j % each),
-    )
+    key = lax.broadcasted_iota(jnp.int32, (128, panel), 0)
+    groups = lax.broadcasted_iota(jnp.int32, (128, panel), 1)
+    chosen = jnp.where(
+        groups == key // each * per_src + each * rcv + key % each, 1.0, 0.0
+    ).astype(bf)
+    mine = lax.dot_general(
+        chosen, offsets, (((1,), (1,)), ((), ())), preferred_element_type=f32
+    )[:, :1].astype(jnp.int32)
+    cells = lax.broadcasted_iota(jnp.int32, (128, rcv_cols), 1)
+    key = lax.broadcasted_iota(jnp.int32, (128, 1), 0)
+    cell = key // each * run_len + STRIDE * (key % each) + mine
+    cell = jnp.where(key < srcs * each, cell, -1)
+    col_pick[...] = jnp.where(cells == cell, 1.0, 0.0).astype(bf)
     pick_from(row_pick, per_src, lambda j: per_src * src + j, lambda j: STRIDE * j)
 
     for chan in range(2):
@@ -417,11 +454,11 @@
 
     fronts, behinds = [], []
     for chan in range(2):
-        picked = lax.dot_general(
-            rec[chan], col_pick[...], (((0,), (0,)), ((), ())), preferred_element_type=f32
-        ).astype(bf)
+        picked = jnp.transpose(jnp.dot(col_pick[...], rec[chan], preferred_element_type=f32))
         for peer in range(rcvs):
-            front_tx[peer, chan] = picked[peer * run_len : (peer + 1) * run_len]
+            front_tx[peer, chan] = pack_traces(
+                picked[peer * run_len : (peer + 1) * run_len]
+            ).astype(bf)
         for index, peer in enumerate(rcv_peers):
             copy = remote(
                 front_tx.at[peer, chan], front_rx.at[rcv, chan], front_send.at[chan, index],
@@ -443,12 +480,11 @@
             behinds.append(copy)
         behind_rx[src, chan] = behind_tx[src, chan]
 
-    keys = srcs * each
     for peer in range(rcvs):
-        index = lax.broadcasted_iota(jnp.int32, (keys, panel), 0)
-        column = lax.broadcasted_iota(jnp.int32, (keys, panel), 1)
+        index = lax.broadcasted_iota(jnp.int32, (128, panel), 0)
+        column = lax.broadcasted_iota(jnp.int32, (128, panel), 1)
         aim = index // each * (rcvs * each) + peer * each + index % each
-        picks[peer * keys : (peer + 1) * keys] = jnp.where(column == aim, 1.0, 0.0).astype(bf)
+        picks[peer * 128 : (peer + 1) * 128] = jnp.where(column == aim, 1.0, 0.0).astype(bf)
 
     heads.wait()
     tails.wait()
@@ -459,6 +495,7 @@
         tile = buffer[chan, run // 2 * 16 : run // 2 * 16 + 16].astype(f32)
         return tile[run % 2 * HALO : run % 2 * HALO + HALO]
 
+    packs = [jnp.zeros((rows, 128), f32), jnp.zeros((rows, 128), f32)]
     for chan in range(2):
         for run in range(srcs):
             below = jnp.where(last_rcv, edge(head_rx, chan, run + 1), edge(head_rx, chan, run))
@@ -466,10 +503,15 @@
             rim = jnp.concatenate([below, above], axis=0).astype(bf)
             rims[chan, run] = rim
             main = slice(run * run_len, (run + 1) * run_len)
-            first_tx[chan, run, :run_len] = rec[chan, main, :128]
-            first_tx[chan, run, run_len:] = rim[:, :128]
-            last_tx[chan, run, :run_len] = rec[chan, main, src_rows - 128 :]
-            last_tx[chan, run, run_len:] = rim[:, src_rows - 128 :]
+            slot = chan * srcs + run
+            for block, lanes in enumerate((slice(0, 128), slice(src_rows - 128, src_rows))):
+                side = jnp.concatenate(
+                    [rec[chan, main, lanes].astype(f32), rim[:, lanes].astype(f32)], axis=0
+                )
+                moved = roll(side, HALO * slot + HALO * block)
+                packs[block] = jnp.where(lanes_of(side) // HALO == slot, moved, packs[block])
+    first_tx[...] = packs[0].astype(bf)
+    last_tx[...] = packs[1].astype(bf)
 
     low = jnp.maximum(src - 1, 0)
     high = jnp.minimum(src + 1, srcs - 1)
@@ -517,12 +559,11 @@
                 behind_tx.at[peer, chan], behind_rx.at[peer, chan], behind_send.at[chan, index],
                 behind_recv.at[chan, peer], (peer, rcv),
             ).wait_recv()
-        total = jnp.zeros((run_len, panel), f32)
         for peer in range(rcvs):
-            total = total + jnp.dot(
-                front_rx[peer, chan], picks[peer * keys : (peer + 1) * keys],
-                preferred_element_type=f32,
-            )
+            gathered[:, peer * 128 : (peer + 1) * 128] = unpack_traces(
+                front_rx[peer, chan].astype(f32)
+            ).astype(bf)
+        total = jnp.dot(gathered[...], picks[...], preferred_element_type=f32)
         for peer in range(srcs):
             shape = (rcvs * each, panel)
             index = lax.broadcasted_iota(jnp.int32, shape, 0)
@@ -660,6 +701,15 @@
             for run in range(srcs):
                 set_right(run)
             tiles_when(lambda gap: gap < spots - 1)
+            for holds, start, which in rim_ends:
+
+                @pl.when(jnp.logical_not(holds))
+                def _():
+                    for chan in range(2):
+                        rim_copy(start, chan, 0, which, rcv).wait_recv()
+
+            multiply(src_rows, 128)
+            out_copy(src_rows, 128, spots).start()
         for chan in range(2):
             for up in (True, False):
                 owner_spot = spot - step if up else spot + step
@@ -679,15 +729,6 @@
 
                     hand(owner, block, chan).start()
 
-    for holds, start, which in rim_ends:
-
-        @pl.when(jnp.logical_not(holds))
-        def _():
-            for chan in range(2):
-                rim_copy(start, chan, 0, which, rcv).wait_recv()
-
-    multiply(src_rows, 128)
-    out_copy(src_rows, 128, spots).start()
     tiles_when(lambda gap: gap == spots - 1)
 
     for copy in fronts + behinds:
@@ -711,13 +752,16 @@
     def _():
         after_rx[...] = jnp.zeros_like(after_rx)
 
-    lane = lax.broadcasted_iota(jnp.int32, (rows, 128), 1)
-    zero = jnp.zeros((rows, 128), bf)
+    after, before = after_rx[...].astype(f32), before_rx[...].astype(f32)
+    lane = lanes_of(after)
+    zero = jnp.zeros((rows, 128), f32)
     for chan in range(2):
         for run in range(srcs):
+            slot = chan * srcs + run
+            high_side = jnp.where(lane >= 128 - HALO, roll(before, 128 - HALO - HALO * slot), zero)
             sides[chan, run] = jnp.where(
-                lane < HALO, after_rx[chan, run], jnp.where(lane >= 128 - HALO, before_rx[chan, run], zero)
-            )
+                lane < HALO, roll(after, -HALO * slot), high_side
+            ).astype(bf)
 
     for chan in range(2):
 
@@ -765,12 +809,13 @@
     each = panel // (srcs * rcvs)
     bf = jnp.bfloat16
     vmem = pl.BlockSpec(memory_space=pltpu.VMEM)
-    front = (rcvs, 2, run_len, srcs * each)
+    front = (rcvs, 2, run_len * 3 // 4, 128)
     behind = (srcs, 2, run_len, rcvs * each)
     edges = (2, HALO * srcs, src_rows)
     side = (2, srcs, rows, 128)
-    shapes = [front, front, behind, behind, edges, edges, edges, edges, side, side, side, side]
-    shapes += [(2, rows, panel), (2, 16, panel), (2, 16, panel), (panel, panel)]
+    pack = (rows, 128)
+    shapes = [front, front, behind, behind, edges, edges, edges, edges, pack, pack, pack, pack]
+    shapes += [(2, rows, panel), (2, 16, panel), (2, 16, panel), (rcvs * 128, panel)]
     shapes += [(src_rows + 128, 2 * panel), (srcs, 2, rows, panel), (2 * srcs * rows, 2 * panel)]
     wide = (2, srcs, rows, src_rows + 128)
     dma = pltpu.SemaphoreType.DMA
@@ -786,8 +831,9 @@
         scratch_shapes=[pltpu.VMEM(shape, bf) for shape in shapes]
         + [
             pltpu.VMEM(wide, jnp.float32),
-            pltpu.VMEM((rcv_cols, srcs * each), bf),
+            pltpu.VMEM((128, rcv_cols), bf),
             pltpu.VMEM((src_rows, rcvs * each), bf),
+            pltpu.VMEM((run_len, rcvs * 128), bf),
         ]
         + [
             dma((2, rcvs)), dma((2, rcvs)), dma((2, srcs)), dma((2, srcs)), dma((8,)), dma((8,)),
@@ -808,7 +854,7 @@
     rcv_count = lax.axis_size("rcv")
     freqs, _, rcv_cols, src_rows = record.shape
     run_len = rcv_cols // src_count
-    if freqs != 1 or run_len % 16 or src_rows % 128 or src_count % 2 or rcv_count % 2 or run_len % 64 or rcv_count < 4:
+    if freqs != 1 or run_len % 16 or src_rows % 128 or src_count % 2 or rcv_count % 2 or run_len % 64 or rcv_count < 4 or src_count * run_len > 96 * STRIDE or src_count * HALO > 64:
         return plain_shards(record, panel_offset)
     pred, rims, sides = exchange_call(record[0], panel_offset, src_count, rcv_count)
     return sweep_call(record, rims, sides, pred, panel_offset.shape[0])

time: 130 us -> 127 us (0.977)
  Pallas kernels: 128 us -> 125 us
    pallas_call x1, Pallas kernels: 90.4 us -> 87.3 us  [exchange_call(): pl.pallas_call(functools.partial(exchange_kernel, (srcs, rcvs)), out_shap...]
where the time goes in v5:
time: 127 us; the launch traced here: 126 us
  Pallas kernels  125 us (98%)
  local copies, waits for them, and re-layouts  1.27 us (1%)
    pallas_call x1, Pallas kernels, exchange_call(): pl.pallas_call(functools.partial(exchange_kernel, (srcs, rcvs)), out_shap...  87.3 us
    pallas_call x1, Pallas kernels, sweep_call(): pl.pallas_call(functools.partial(sweep_kernel, panel ** (-0.5)), grid=(ru...  37.2 us

profile of v5, /device:TPU:0, one launch (start us, length us, event | category | flops | bytes accessed | tf_op | source)
XLA Modules:
  0.0 126.5 jit_solution(11375601049662206912)
XLA Ops:
  0.6 1.3 %reshape.7.offset = s32[1,768]{1,0:T(1,128)} reshape(s32[768]{0:T(1024)} %param.3) | data formatting | bytes 6144 | tf_op jit(solution)/shard_map/reshape | solution.py:849
  1.9 87.3 %shard_map.41 = (f32[2,4,208,1664]{3,2,1,0:T(8,128)}, bf16[2,4,16,1536]{3,2,1,0:T(8,128)(2,1)}, bf16[2,4,208,128]{3,2,1,0:T(8,128)(2,1)}) custom-call(bf16[2,768,1536]{2,1,0:T(8,128)(2,1)} %bitcast.1, s32[1,768]{1,0:T(1,128)} %reshape.7.offset), custom_call_target="tpu_custom_call" | custom-call | flops 10000000000 | bytes 18874368 | tf_op jit(solution)/shard_map/pallas_call | solution.py:822
  89.3 37.2 %shard_map.42 = (bf16[1,2,768,1536]{3,2,1,0:T(8,128)(2,1)}, bf16[1,2,768,1536]{3,2,1,0:T(8,128)(2,1)}) custom-call(bf16[1,2,768,1536]{3,2,1,0:T(8,128)(2,1)} %record_ref.1, bf16[2,4,16,1536]{3,2,1,0:T(8,128)(2,1)} %get-tuple-element.5.rim_ref, bf16[2,4,208,128]{3,2,1,0:T(8,128)(2,1)} %get-tuple-element.6.side_ref, f32[2,4,208,1664]{3,2,1,0:T(8,128)} %get-tuple-element.7.pred_ref), custom_call_target="tpu_custom_call" | custom-call | flops 12000000000 | bytes 18874368 | tf_op jit(solution)/shard_map/pallas_call | solution.py:293

commit v6 on v5

--- a/solution.py
+++ b/solution.py
@@ -215,9 +215,10 @@
     def new_err(at, lanes):
         here = [data[chan, at, lanes].astype(f32) for chan in range(2)]
         guess = [predb[chan, at, lanes].astype(f32) for chan in range(2)]
-        inverse = 1.0 / (totals[2, at, lanes] + weight_eps)
-        gain_real = totals[0, at, lanes] * inverse
-        gain_imag = totals[1, at, lanes] * inverse
+        sums = [totals[pl.ds(index * rows + at.start, at.size), lanes] for index in range(3)]
+        inverse = 1.0 / (sums[2] + weight_eps)
+        gain_real = sums[0] * inverse
+        gain_imag = sums[1] * inverse
         err = (
             here[0] - (gain_real * guess[0] - gain_imag * guess[1]),
             here[1] - (gain_real * guess[1] + gain_imag * guess[0]),
@@ -226,19 +227,19 @@
 
     def box():
         for index in range(3):
+            part = slice(index * rows, (index + 1) * rows)
             for start, size in wide_spans(width):
-                partial[index, :, 128 + start : 128 + start + size] = jnp.dot(
+                partial[part, 128 + start : 128 + start + size] = jnp.dot(
                     row_band[...], terms[index, :, start : start + size], preferred_element_type=f32
                 ).astype(bf)
-            partial[index, :, :128] = partial[index, :, width : width + 128]
-            partial[index, :, width + 128 :] = partial[index, :, 128:256]
-        for index in range(3):
-            for start, size in wide_spans(width):
-                totals[index, :, start : start + size] = jnp.dot(
-                    partial[index, :, start : start + size + 256],
-                    lane_band[: size + 256, :size],
-                    preferred_element_type=f32,
-                )
+        partial[:, :128] = partial[:, width : width + 128]
+        partial[:, width + 128 :] = partial[:, 128:256]
+        for start, size in wide_spans(width):
+            totals[:, start : start + size] = jnp.dot(
+                partial[:, start : start + size + 256],
+                lane_band[: size + 256, :size],
+                preferred_element_type=f32,
+            )
 
     @pl.loop(0, rows // 16)
     def _(step):
@@ -305,8 +306,8 @@
             pltpu.VMEM((2, rows, width), bf),
             pltpu.VMEM((2, rows, width), bf),
             pltpu.VMEM((3, rows, width), bf),
-            pltpu.VMEM((3, rows, width + 256), bf),
-            pltpu.VMEM((3, rows, width), f32),
+            pltpu.VMEM((3 * rows, width + 256), bf),
+            pltpu.VMEM((3 * rows, width), f32),
             pltpu.VMEM((rows, rows), bf),
             pltpu.VMEM((512, 256), bf),
         ],
@@ -402,7 +403,7 @@
     def _():
         pl.semaphore_signal(barrier, inc=1, device_id=prev_dev, device_id_type=MESH)
 
-    offsets = jnp.broadcast_to(offset[...].astype(f32), (8, panel)).astype(bf)
+    offsets = jnp.broadcast_to(offset[...].astype(f32).reshape(1, panel), (8, panel)).astype(bf)
 
     def pick_from(target, count, group_of, cell_of):
         groups = lax.broadcasted_iota(jnp.int32, (panel, count), 0)
@@ -545,6 +546,15 @@
             pl.ds(pl.multiple_of(owner * run_len, 16), run_len), pl.ds(chan * panel, panel)
         ]
 
+    def right_copy(kind, index, slot, peer):
+        rims_only = kind == 2
+        at = pl.ds(run_len, 2 * HALO) if rims_only else pl.ds(0, run_len)
+        chans = pl.ds(0, 2) if rims_only else pl.ds(kind, 1)
+        return remote(
+            own.at[chans, at], right.at[slot, chans, at], right_send.at[kind, index],
+            right_recv.at[kind, slot], (peer, rcv),
+        )
+
     to_prev, to_next = [], []
     for chan in range(2):
         for index, step in enumerate(range(1, rcvs)):
@@ -582,6 +592,8 @@
             line(spot, mine, False, 0, chan).start()
 
         hand(rcv, mine, chan).start()
+        for index, peer in enumerate(src_peers):
+            right_copy(chan, index, src, peer).start()
         to_prev.append(
             remote(
                 own.at[chan, pl.ds(0, 16)], next_rx.at[chan], edge_send.at[4 + chan],
@@ -627,11 +639,8 @@
 
     place = lax.broadcasted_iota(jnp.int32, (2, 2 * HALO, panel), 1)
     own[:, run_len:] = jnp.where(place < HALO, next_rx[...], prev_rx[...])
-    rights = []
     for index, peer in enumerate(src_peers):
-        copy = remote(own, right.at[src], right_send.at[index], right_recv.at[src], (peer, rcv))
-        copy.start()
-        rights.append(copy)
+        right_copy(2, index, src, peer).start()
     right[src] = own[...]
 
     def rim_copy(start, chan, index, which, peer):
@@ -695,9 +704,8 @@
         if step == spots - 1:
             for other in range(1, srcs):
                 peer = lax.rem(src + srcs - other, srcs)
-                remote(
-                    own, right.at[peer], right_send.at[0], right_recv.at[peer], (peer, rcv)
-                ).wait_recv()
+                for kind in range(3):
+                    right_copy(kind, 0, peer, peer).wait_recv()
             for run in range(srcs):
                 set_right(run)
             tiles_when(lambda gap: gap < spots - 1)
@@ -794,8 +802,9 @@
         for index in range(spots):
             hand(2 * index + core, mine, chan).wait_send()
 
-    for copy in rights:
-        copy.wait_send()
+    for kind in range(3):
+        for index, peer in enumerate(src_peers):
+            right_copy(kind, index, src, peer).wait_send()
     for index in range(spots):
         out_copy(index * span, span, index).wait()
     out_copy(src_rows, 128, spots).wait()
@@ -837,7 +846,7 @@
         ]
         + [
             dma((2, rcvs)), dma((2, rcvs)), dma((2, srcs)), dma((2, srcs)), dma((8,)), dma((8,)),
-            dma((srcs,)), dma((srcs,)), dma((2, 2, rcvs // 2)), dma((2, rcvs)), dma((2, rcvs // 2)),
+            dma((3, srcs)), dma((3, srcs)), dma((2, 2, rcvs // 2)), dma((2, rcvs)), dma((2, rcvs // 2)),
             dma((2, rcvs)), dma((2, 2)), dma((rcvs // 2 + 1,)),
         ],
         compiler_params=pltpu.CompilerParams(
@@ -846,7 +855,7 @@
         cost_estimate=pl.CostEstimate(
             flops=10_000_000_000, bytes_accessed=8 * rec.size, transcendentals=0
         ),
-    )(rec, panel_offset.reshape(1, panel))
+    )(rec, panel_offset)
 
 
 def shards(record, panel_offset):

time: 127 us -> 118 us (0.929)
  Pallas kernels: 125 us -> 117 us
  local copies, waits for them, and re-layouts: 1.27 us -> 0 us
    pallas_call x1, Pallas kernels: 87.3 us -> 77.6 us  [exchange_call(): pl.pallas_call(functools.partial(exchange_kernel, (srcs, rcvs)), out_shap...]
    pallas_call x1, Pallas kernels: 37.2 us -> 39.8 us  [sweep_call(): pl.pallas_call(functools.partial(sweep_kernel, panel ** (-0.5)), grid=(ru...]
where the time goes in v6:
time: 118 us
  Pallas kernels  117 us (99%)
    pallas_call x1, Pallas kernels, exchange_call(): pl.pallas_call(functools.partial(exchange_kernel, (srcs, rcvs)), out_shap...  77.6 us
    pallas_call x1, Pallas kernels, sweep_call(): pl.pallas_call(functools.partial(sweep_kernel, panel ** (-0.5)), grid=(ru...  39.8 us

profile of v6, /device:TPU:0, one launch (start us, length us, event | category | flops | bytes accessed | tf_op | source)
XLA Modules:
  0.0 118.0 jit_solution(7177404277159700492)
XLA Ops:
  0.6 77.6 %shard_map.41 = (f32[2,4,208,1664]{3,2,1,0:T(8,128)}, bf16[2,4,16,1536]{3,2,1,0:T(8,128)(2,1)}, bf16[2,4,208,128]{3,2,1,0:T(8,128)(2,1)}) custom-call(bf16[2,768,1536]{2,1,0:T(8,128)(2,1)} %bitcast.1, s32[768]{0:T(1024)} %offset.1), custom_call_target="tpu_custom_call" | custom-call | flops 10000000000 | bytes 18874368 | tf_op jit(solution)/shard_map/pallas_call | solution.py:831
  78.2 39.8 %shard_map.42 = (bf16[1,2,768,1536]{3,2,1,0:T(8,128)(2,1)}, bf16[1,2,768,1536]{3,2,1,0:T(8,128)(2,1)}) custom-call(bf16[1,2,768,1536]{3,2,1,0:T(8,128)(2,1)} %record_ref.1, bf16[2,4,16,1536]{3,2,1,0:T(8,128)(2,1)} %get-tuple-element.5.rim_ref, bf16[2,4,208,128]{3,2,1,0:T(8,128)(2,1)} %get-tuple-element.6.side_ref, f32[2,4,208,1664]{3,2,1,0:T(8,128)} %get-tuple-element.7.pred_ref), custom_call_target="tpu_custom_call" | custom-call | flops 12000000000 | bytes 18874368 | tf_op jit(solution)/shard_map/pallas_call | solution.py:294
